TPU v7x, 512 devices: a whole 4x4x16 slice. The times are simulated.
512 devices in a mesh: seq: 32 (over z, core), head: 16 (over x, y).
Axes of the slice: x: 4, y: 4, z: 16, core: 2. Of those that a mesh axis runs over, the one named last changes fastest.
Arguments:
- conv_output: bfloat16 [4096, 8192], P('seq', 'head'), may hold values from -6 to 6
- output_grad: bfloat16 [4096, 8192], P('seq', 'head'), may hold values from -6 to 6
- write_keys: bfloat16 [4096, 2048], P('seq', 'head'), may hold values from -1.5 to 1.5
- read_queries: bfloat16 [4096, 2048], P('seq', 'head'), may hold values from -1.5 to 1.5
- log_decay: float32 [4096, 128], P('seq', 'head'), may hold values from -0.7 to 0
- step_size: float32 [4096, 128], P('seq', 'head'), may hold values from 0.005 to 0.05
- skip_gain: float32 [128], P('head'), may hold values from 0.5 to 1.5
- conv_weight: float32 [4, 8192], P(None, 'head'), may hold values from -3 to 3
Outputs:
- input_grad: bfloat16 [4096, 8192], P('seq', 'head')
- keys_grad: float32 [4096, 2048], P('seq', 'head')
- queries_grad: float32 [4096, 2048], P('seq', 'head')
- decay_grad: float32 [4096, 128], P('seq', 'head')
- step_grad: float32 [4096, 128], P('seq', 'head')
All inputs are finite; a program needn't handle non-finite values.
Results may differ from a plain program's by a relative error of at most 0.0055.
Values may be sent and summed in bfloat16 or wider, within the bound.
A program may use at most 64 MiB of HBM per device.

v0:
```python
import jax
import jax.numpy as jnp
from jax import lax
from jax.sharding import PartitionSpec as P

precise = lax.Precision.HIGHEST


def swapped(block, axis, bit):
    count = lax.axis_size(axis)
    route = []
    for low in range(count):
        high = low | 1 << bit
        if high != low and high < count:
            route += [(low, high), (high, low)]
    return lax.ppermute(block, axis, route)


def carried_in(shard, axis, combine, identity, reverse):
    peers, place = (lax.axis_size(axis), lax.axis_index(axis))
    everything = jax.tree.map(lambda part: lax.all_gather(part, axis), shard)
    start = jax.tree.map(
        lambda part, zero: jnp.broadcast_to(jnp.asarray(zero, part.dtype), part.shape),
        shard,
        identity,
    )

    def lap(k, before):
        at = peers - 1 - k if reverse else k
        reached = at > place if reverse else at < place
        new = combine(before, jax.tree.map(lambda part: part[at], everything))
        return jax.tree.map(lambda a, b: jnp.where(reached, a, b), new, before)

    return lax.fori_loop(0, peers, lap, start)


def shifted(block, axis, distance):
    devices = range(lax.axis_size(axis))
    route = [(i - distance, i) for i in devices if i - distance in devices]
    return lax.ppermute(block, axis, route)


def product(left, right):
    return jnp.dot(left, right, preferred_element_type=jnp.float32, precision=precise)


def forward_combine(earlier, latter):
    return (earlier[0] * latter[0], latter[0][:, None, None] * earlier[1] + latter[1])


def backward_combine(earlier, latter):
    return (latter[0] * earlier[0], latter[1] + latter[0][:, None, None] * earlier[1])


def body(
    conv_output, output_grad, write_keys, read_queries, log_decay, step_size, skip_gain, conv_weight
):
    length = conv_output.shape[0]
    head_count = log_decay.shape[1]
    head_width = conv_output.shape[1] // head_count
    parity = lax.axis_index("head") % 2
    own_first = parity == 0
    partner = swapped((write_keys, read_queries), "head", 0)
    keys_full = jnp.where(
        own_first,
        jnp.concatenate([write_keys, partner[0]], 1),
        jnp.concatenate([partner[0], write_keys], 1),
    ).astype(jnp.float32)
    queries_full = jnp.where(
        own_first,
        jnp.concatenate([read_queries, partner[1]], 1),
        jnp.concatenate([partner[1], read_queries], 1),
    ).astype(jnp.float32)
    state_count = keys_full.shape[1]
    preact = conv_output.astype(jnp.float32)
    values = jax.nn.silu(preact)
    upstream = output_grad.astype(jnp.float32)
    values3 = values.reshape(length, head_count, head_width)
    upstream3 = upstream.reshape(length, head_count, head_width)
    cumulative = jnp.cumsum(log_decay, axis=0)
    totals = cumulative[-1]
    to_end = jnp.exp(totals[None, :] - cumulative)
    from_start = jnp.exp(cumulative)
    weighted = values3 * (to_end * step_size)[:, :, None]
    seeded = upstream3 * from_start[:, :, None]
    local_state = jnp.einsum("ln,lhp->hnp", keys_full, weighted, precision=precise)
    local_grad = jnp.einsum("ln,lhp->hnp", queries_full, seeded, precision=precise)
    decay_total = jnp.exp(totals)
    identity = (jnp.ones_like(decay_total), jnp.zeros_like(local_state))
    entering = carried_in((decay_total, local_state), "seq", forward_combine, identity, False)[1]
    arriving = carried_in((decay_total, local_grad), "seq", backward_combine, identity, True)[1]
    scores = product(queries_full, keys_full.T)
    row_ids = lax.broadcasted_iota(jnp.int32, (length, length), 0)
    col_ids = lax.broadcasted_iota(jnp.int32, (length, length), 1)
    causal = row_ids >= col_ids
    cum_heads = cumulative.T
    step_heads = step_size.T
    log_gap = jnp.where(causal[None], cum_heads[:, :, None] - cum_heads[:, None, :], -1e30)
    decay_mask = jnp.exp(log_gap)
    pair_dots = jnp.einsum("thp,shp->hts", upstream3, values3, precision=precise)
    masked_scores = decay_mask * scores[None]
    weight_sum = jnp.einsum("hts,hs->ts", decay_mask * pair_dots, step_heads, precision=precise)
    within = jnp.einsum(
        "hts,thp->shp", masked_scores * step_heads[:, None, :], upstream3, precision=precise
    )
    effect = masked_scores * pair_dots
    row_sums = jnp.einsum("hts,hs->th", effect, step_heads, precision=precise)
    col_sums = jnp.sum(effect, 1).T
    from_state = jnp.einsum("ln,hnp->lhp", queries_full, entering, precision=precise)
    into_state = jnp.einsum("ln,hnp->lhp", keys_full, arriving, precision=precise)
    carried = jnp.sum(values3 * into_state, 2)
    step_grad = col_sums + to_end * carried
    value_grad = (
        within
        + skip_gain[None, :, None] * upstream3
        + (to_end * step_size)[:, :, None] * into_state
    )
    leaving = decay_total[:, None, None] * entering + local_state
    decay_terms = (
        row_sums
        - col_sums * step_size
        + from_start * jnp.sum(upstream3 * from_state, 2)
        - to_end * step_size * carried
    )
    last_row = (lax.broadcasted_iota(jnp.int32, (length, 1), 0) == length - 1).astype(jnp.float32)
    decay_terms = decay_terms + last_row * jnp.sum(arriving * leaving, (1, 2))[None, :]
    decay_grad = jnp.flip(jnp.cumsum(jnp.flip(decay_terms, 0), 0), 0)
    query_part = product(weight_sum, keys_full) + jnp.einsum(
        "lhp,hnp->ln", seeded, entering, precision=precise
    )
    key_part = lax.dot_general(
        weight_sum,
        queries_full,
        (((0,), (0,)), ((), ())),
        preferred_element_type=jnp.float32,
        precision=precise,
    )
    key_part = key_part + jnp.einsum("lhp,hnp->ln", weighted, arriving, precision=precise)
    half_width = state_count // 2
    key_mine = jnp.where(own_first, key_part[:, :half_width], key_part[:, half_width:])
    key_other = jnp.where(own_first, key_part[:, half_width:], key_part[:, :half_width])
    query_mine = jnp.where(own_first, query_part[:, :half_width], query_part[:, half_width:])
    query_other = jnp.where(own_first, query_part[:, half_width:], query_part[:, :half_width])
    received = (
        swapped(key_other.astype(jnp.bfloat16), "head", 0).astype(key_other.dtype),
        swapped(query_other.astype(jnp.bfloat16), "head", 0).astype(query_other.dtype),
    )
    keys_grad = key_mine + received[0]
    queries_grad = query_mine + received[1]
    logistic = jax.nn.sigmoid(preact)
    conv_grad = value_grad.reshape(length, -1) * logistic * (1.0 + preact * (1.0 - logistic))
    following = shifted(conv_grad[:3], "seq", -1)
    extended = jnp.concatenate([conv_grad, following], 0)
    input_grad = jnp.zeros_like(conv_grad)
    for offset in range(4):
        input_grad = (
            input_grad + conv_weight[offset][None, :] * extended[3 - offset : 3 - offset + length]
        )
    return (input_grad.astype(jnp.bfloat16), keys_grad, queries_grad, decay_grad, step_grad)


def solution(mesh):
    return jax.shard_map(
        body,
        mesh=mesh,
        in_specs=(
            P("seq", "head"),
            P("seq", "head"),
            P("seq", "head"),
            P("seq", "head"),
            P("seq", "head"),
            P("seq", "head"),
            P("head"),
            P(None, "head"),
        ),
        out_specs=(
            P("seq", "head"),
            P("seq", "head"),
            P("seq", "head"),
            P("seq", "head"),
            P("seq", "head"),
        ),
        check_vma=False,
    )
```

profile of v0, /device:TPU:1, one launch (start us, length us, event | category | flops | bytes accessed | tf_op | source)
XLA Modules:
  0.0 395.1 jit_solution(6024814424454256812)
XLA Ops:
  7.2 4.0 %collective-permute-start = (bf16[128,128]{1,0:T(8,128)(2,1)}, bf16[128,128]{1,0:T(8,128)(2,1)S(1)}, u32[]{:S(2)}, u32[]{:S(2)}) collective-permute-start(bf16[128,128]{1,0:T(8,128)(2,1)} %param.15), channel_id=1, source_target_pairs={{0,1},{1,0},{2,3},{3,2},{4,5},{5,4},{6,7},{7,6},{8,9},{9,8},{10,11... | collective-permute-start | bytes 98312 | tf_op jit(solution)/shard_map/ppermute | solution.py:16
  14.7 2.0 convolution_bitcast_fusion.2
  16.8 1.9 collective-permute-start.1
  18.9 37.4 %all-gather.2 = f32[32,1,8]{2,1,0:T(1,128)S(1)} all-gather(f32[1,1,8]{2,1,0:T(1,128)S(1)} %get-tuple-element.326), channel_id=1, replica_groups=mesh['seq'=32,'head'=16] {'seq'}, dimensions={0}, use_global_device_ids=true | all-gather | bytes 1056 | tf_op jit(solution)/shard_map/all_gather | solution.py:21
  57.4 71.3 %all-gather.6.cloned.1.call-done = f32[256,256,64]{1,2,0:T(8,128)} async-done(((f32[8,256,64]{1,2,0:T(8,128)}), f32[256,256,64]{1,2,0:T(8,128)}) %all-gather.6.cloned.1.call-update) | async-done | bytes 16777232 | tf_op jit(solution)/shard_map/all_gather | solution.py:21
  128.7 58.9 %while.30 = (s32[]{:T(128)}, f32[8,256,64]{2,1,0:T(8,128)S(1)}, s32[]{:T(128)}, f32[32,8,256,64]{2,3,1,0:T(8,128)}, f32[32,8]{1,0:T(8,128)S(1)}, /*index=5*/s32[]{:T(128)}, s32[]{:T(128)}, s32[]{:T(128)}, s32[]{:T(128)}) while((s32[]{:T(128)}, f32[8,256,64]{2,1,0:T(8,128)S(1)}, s32[]{:T(128)}, f32[32,8,256,64]{2,3,1,0:T(8,128)}, ...), condition=%wide.region_2.3_spmd.clone, body=%wide.region_1.2_spmd.clone.sunk | while | flops 524296 | bytes 3670287 | solution.py:34
  128.7 1.1 constant_dynamic-slice_fusion.4
  134.2 1.1 constant_dynamic-slice_fusion.4
  139.8 1.1 constant_dynamic-slice_fusion.4
  145.3 1.1 constant_dynamic-slice_fusion.4
  152.6 1.1 constant_dynamic-slice_fusion.4
  158.2 1.1 constant_dynamic-slice_fusion.4
  163.7 1.1 constant_dynamic-slice_fusion.4
  169.2 1.1 constant_dynamic-slice_fusion.4
  189.3 2.0 convolution_bitcast_fusion
  191.9 1.3 fusion.51
  193.2 1.4 fusion.55
  195.2 2.2 collective-permute-start.2
  197.4 1.3 multiply_reduce_fusion
  198.7 1.7 fusion.8
  200.4 1.7 convolution_bitcast_fusion.5
  202.1 1.1 convolution_add_fusion.1
  203.2 1.9 fusion.9
  205.9 3.1 collective-permute-start.3
  209.0 1.4 copy.47
  211.2 1.6 fusion.16
  213.4 82.7 %all-gather.8.cloned.1.call-done = f32[256,256,64]{1,2,0:T(8,128)} async-done(((f32[8,256,64]{1,2,0:T(8,128)}), f32[256,256,64]{1,2,0:T(8,128)}) %all-gather.8.cloned.1.call-update) | async-done | bytes 16777232 | tf_op jit(solution)/shard_map/all_gather | solution.py:21
  296.2 80.0 %while.31 = (s32[]{:T(128)}, f32[8,256,64]{2,1,0:T(8,128)S(1)}, s32[]{:T(128)}, f32[32,8]{1,0:T(8,128)}, f32[32,8,256,64]{2,3,1,0:T(8,128)}, /*index=5*/s32[]{:T(128)}, s32[]{:T(128)}) while((s32[]{:T(128)}, f32[8,256,64]{2,1,0:T(8,128)S(1)}, s32[]{:T(128)}, f32[32,8]{1,0:T(8,128)}, f32[32,8,256,64]{2,3,1,0:T(8,128)}, ...), condition=%wide.region_4.5_spmd.clone, body=%wide.region_3.4_spmd.clone.sunk | while | flops 524292 | bytes 3670225 | solution.py:34
  376.2 1.7 convolution_bitcast_fusion.4
  378.2 1.3 multiply_reduce_fusion.1
  379.5 1.2 fusion.19
  382.0 3.1 collective-permute-start.4
  (342 shorter events, 141.1 us)
Async XLA Ops:
  7.2 180.8 %copy-start.7 = (bf16[128,128]{1,0:T(8,128)(2,1)S(1)}, bf16[128,128]{1,0:T(8,128)(2,1)}, u32[]{:S(2)}) copy-start(bf16[128,128]{1,0:T(8,128)(2,1)} %param.14) | copy-start | bytes 98308
  7.2 121.5 %all-gather.6.cloned.1.call-start = ((), (), s32[]{:S(2)}) async-start(), calls=%async_computation | async-start | bytes 17301504 | tf_op jit(solution)/shard_map/all_gather | solution.py:21
  7.2 7.5 %collective-permute-start = (bf16[128,128]{1,0:T(8,128)(2,1)}, bf16[128,128]{1,0:T(8,128)(2,1)S(1)}, u32[]{:S(2)}, u32[]{:S(2)}) collective-permute-start(bf16[128,128]{1,0:T(8,128)(2,1)} %param.15), channel_id=1, source_target_pairs={{0,1},{1,0},{2,3},{3,2},{4,5},{5,4},{6,7},{7,6},{8,9},{9,8},{10,11... | collective-permute-start | bytes 98312 | tf_op jit(solution)/shard_map/ppermute | solution.py:16
  12.1 1.1 copy-start.2
  13.0 115.6 %copy-start = (f32[128,8]{1,0:T(8,128)}, f32[128,8]{1,0:T(8,128)S(1)}, u32[]{:S(2)}) copy-start(f32[128,8]{1,0:T(8,128)S(1)} %reduce_window_sum.18) | copy-start | bytes 12292
  13.1 0.6 copy-start.19
  13.1 115.6 %copy-start.4 = (f32[128,8]{1,0:T(8,128)}, f32[128,8]{1,0:T(8,128)S(1)}, u32[]{:S(2)}) copy-start(f32[128,8]{1,0:T(8,128)S(1)} %get-tuple-element.323) | copy-start | bytes 12292
  14.7 173.6 %copy-start.18 = (f32[128,8]{0,1:T(8,128)S(1)}, f32[128,8]{0,1:T(8,128)}, u32[]{:S(2)}) copy-start(f32[128,8]{0,1:T(8,128)} %param.17) | copy-start | bytes 12292
  14.7 173.6 %copy-start.23 = (f32[8]{0:T(128)S(1)}, f32[8]{0:T(128)}, u32[]{:S(2)}) copy-start(f32[8]{0:T(128)} %param.18) | copy-start | bytes 100
  14.7 113.9 %copy-start.14 = (f32[128,8]{0,1:T(8,128)}, f32[128,8]{0,1:T(8,128)S(1)}, u32[]{:S(2)}) copy-start(f32[128,8]{0,1:T(8,128)S(1)} %copy.39) | copy-start | bytes 12292
  14.7 113.9 %copy-start.9 = (bf16[128,128]{1,0:T(8,128)(2,1)}, bf16[128,128]{1,0:T(8,128)(2,1)S(1)}, u32[]{:S(2)}) copy-start(bf16[128,128]{1,0:T(8,128)(2,1)S(1)} %collective-permute-done) | copy-start | bytes 98308
  16.8 279.4 %all-gather.8.cloned.1.call-start = ((), (), s32[]{:S(2)}) async-start(), calls=%async_computation.1 | async-start | bytes 17301504 | tf_op jit(solution)/shard_map/all_gather | solution.py:21
  16.8 39.5 %collective-permute-start.1 = (bf16[128,128]{1,0:T(8,128)(2,1)}, bf16[128,128]{1,0:T(8,128)(2,1)S(1)}, u32[]{:S(2)}, u32[]{:S(2)}) collective-permute-start(bf16[128,128]{1,0:T(8,128)(2,1)} %param.14), channel_id=1, source_target_pairs={{0,1},{1,0},{2,3},{3,2},{4,5},{5,4},{6,7},{7,6},{8,9},{9,8},{10,11... | collective-permute-start | bytes 98312 | tf_op jit(solution)/shard_map/ppermute | solution.py:16
  18.9 170.0 %copy-start.15 = (f32[8,128]{1,0:T(8,128)}, f32[8,128]{1,0:T(8,128)S(1)}, u32[]{:S(2)}) copy-start(f32[8,128]{1,0:T(8,128)S(1)} %copy.34) | copy-start | bytes 12292
  18.9 170.0 %copy-start.16 = (f32[128,8]{0,1:T(8,128)}, f32[128,8]{0,1:T(8,128)S(1)}, u32[]{:S(2)}) copy-start(f32[128,8]{0,1:T(8,128)S(1)} %copy.38) | copy-start | bytes 12292
  56.3 132.7 %copy-start.12 = (bf16[128,512]{1,0:T(8,128)(2,1)S(1)}, bf16[128,512]{1,0:T(8,128)(2,1)}, u32[]{:S(2)}) copy-start(bf16[128,512]{1,0:T(8,128)(2,1)} %param.12) | copy-start | bytes 393220
  56.3 132.6 %copy-start.10 = (bf16[128,128]{1,0:T(8,128)(2,1)}, bf16[128,128]{1,0:T(8,128)(2,1)S(1)}, u32[]{:S(2)}) copy-start(bf16[128,128]{1,0:T(8,128)(2,1)S(1)} %collective-permute-done.1) | copy-start | bytes 98308
  57.3 131.6 %copy-start.13 = (f32[128,128]{1,0:T(8,128)}, f32[128,128]{1,0:T(8,128)S(1)}, u32[]{:S(2)}) copy-start(f32[128,128]{1,0:T(8,128)S(1)} %fusion.53) | copy-start | bytes 196612
  187.6 1.6 copy-start.17
  195.2 16.0 %collective-permute-start.2 = (f32[3,512]{1,0:T(4,128)}, f32[3,512]{1,0:T(4,128)}, u32[]{:S(2)}, u32[]{:S(2)}) collective-permute-start(f32[3,512]{1,0:T(4,128)} %slice.57), channel_id=1, source_target_pairs={{16,0},{32,16},{48,32},{64,48},{80,64},{96,80},{112,96},{128,112},... | collective-permute-start | bytes 18440 | tf_op jit(solution)/shard_map/ppermute | solution.py:40
  198.7 6.5 %copy-start.11 = (f32[128,128]{0,1:T(8,128)}, f32[128,128]{0,1:T(8,128)S(1)}, u32[]{:S(2)}) copy-start(f32[128,128]{0,1:T(8,128)S(1)} %get-tuple-element.331) | copy-start | bytes 196612
  205.2 173.1 %copy-start.21 = (f32[8]{0:T(128)S(1)}, f32[8]{0:T(128)}, u32[]{:S(2)}) copy-start(f32[8]{0:T(128)} %fusion.51) | copy-start | bytes 100
  205.9 6.8 %collective-permute-start.3 = (bf16[128,128]{1,0:T(8,128)(2,1)S(1)}, bf16[128,128]{1,0:T(8,128)(2,1)S(1)}, u32[]{:S(2)}, u32[]{:S(2)}) collective-permute-start(bf16[128,128]{1,0:T(8,128)(2,1)S(1)} %select_convert_fusion.1), channel_id=1, source_target_pairs={{0,1},{1,0},{2,3},{3,2},{4,5},{5,4},{6,7},{7,6},{8,9},{9,8},{10,11... | collective-permute-start | bytes 98312 | tf_op jit(solution)/shard_map/ppermute | solution.py:16
  213.4 166.1 %copy-start.6 = (bf16[128,128]{1,0:T(8,128)(2,1)S(1)}, bf16[128,128]{1,0:T(8,128)(2,1)}, u32[]{:S(2)}) copy-start(bf16[128,128]{1,0:T(8,128)(2,1)} %param.15) | copy-start | bytes 98308
  296.2 84.7 %copy-start.8 = (bf16[128,128]{1,0:T(8,128)(2,1)S(1)}, bf16[128,128]{1,0:T(8,128)(2,1)}, u32[]{:S(2)}) copy-start(bf16[128,128]{1,0:T(8,128)(2,1)} %param.14) | copy-start | bytes 98308
  296.2 88.9 %copy-start.1 = (f32[128,8]{1,0:T(8,128)S(1)}, f32[128,8]{1,0:T(8,128)}, u32[]{:S(2)}) copy-start(f32[128,8]{1,0:T(8,128)} %copy-done) | copy-start | bytes 12292
  296.2 88.9 %copy-start.3 = (f32[128,8]{1,0:T(8,128)S(1)}, f32[128,8]{1,0:T(8,128)}, u32[]{:S(2)}) copy-start(f32[128,8]{1,0:T(8,128)} %copy-done.2) | copy-start | bytes 12292
  296.2 88.9 %copy-start.5 = (f32[128,8]{1,0:T(8,128)S(1)}, f32[128,8]{1,0:T(8,128)}, u32[]{:S(2)}) copy-start(f32[128,8]{1,0:T(8,128)} %copy-done.4) | copy-start | bytes 12292
  296.2 88.9 %copy-start.20 = (f32[8]{0:T(128)S(1)}, f32[8]{0:T(128)}, u32[]{:S(2)}) copy-start(f32[8]{0:T(128)} %copy-done.19) | copy-start | bytes 100
  296.2 88.9 %copy-start.22 = (f32[128]{0:T(128)S(1)}, f32[128]{0:T(128)}, u32[]{:S(2)}) copy-start(f32[128]{0:T(128)} %compare_convert_fusion) | copy-start | bytes 1540
  382.0 5.7 %collective-permute-start.4 = (bf16[128,128]{1,0:T(8,128)(2,1)S(1)}, bf16[128,128]{1,0:T(8,128)(2,1)S(1)}, u32[]{:S(2)}, u32[]{:S(2)}) collective-permute-start(bf16[128,128]{1,0:T(8,128)(2,1)S(1)} %select_convert_fusion), channel_id=1, source_target_pairs={{0,1},{1,0},{2,3},{3,2},{4,5},{5,4},{6,7},{7,6},{8,9},{9,8},{10,11... | collective-permute-start | bytes 98312 | tf_op jit(solution)/shard_map/ppermute | solution.py:16
Sparse Core Ops, SparseCore 0:
  16.9 111.7 all-gather.5
  191.5 104.6 all-gather.7
where the time goes:
time: 400 us; the launch traced here: 395 us
  waiting for transfers between devices  154 us (38%)
  local copies, waits for them, and re-layouts  125 us (31%)
  blocking collectives  37.4 us (9%)
  other arithmetic  30.5 us (8%)
  matrix products  16 us (4%)
  between operations  14.5 us (4%)
  starting transfers between devices  14.4 us (4%)
    all_gather x2, waiting for transfers between devices, carried_in(): everything = jax.tree.map(lambda part: lax.all_gather(part, axis), shard)  154 us
    dynamic_slice x128, local copies, waits for them, and re-layouts, lap(): new = combine(before, jax.tree.map(lambda part: part[at], everything))  90.7 us
    all_gather x1, blocking collectives, carried_in(): everything = jax.tree.map(lambda part: lax.all_gather(part, axis), shard)  37.4 us
    select_n x64, other arithmetic, lap(): return jax.tree.map(lambda a, b: jnp.where(reached, a, b), new, before)  22.5 us
    mul x32, local copies, waits for them, and re-layouts, forward_combine(): latter[0][:, None, None] * earlier[1] + latter[1]  22 us
    ppermute x4, starting transfers between devices, swapped(): return lax.ppermute(block, axis, route)  12.2 us
  transfers between devices with their start and end apart: 7, of which 2 were waited for; matrix products, arithmetic and copies ran while one was open for 6% of the time, Pallas kernels for 0%

commit v1 on v0

v1 whole, which is shorter than its diff:
```python
import functools

import jax
import jax.numpy as jnp
from jax import lax
from jax.experimental import pallas as pl
from jax.experimental.pallas import tpu as pltpu
from jax.sharding import PartitionSpec as P

MESH = pl.DeviceIdType.MESH
F32 = jnp.float32
BF16 = jnp.bfloat16
LEN = 128
WIDTH = 512
HEADS = 8
HALF = 128
STATE = 256
CHUNK = 32
CHUNKS = STATE // CHUNK


def dot(a, b):
    return lax.dot_general(a, b, (((1,), (0,)), ((), ())), preferred_element_type=F32)


def dot_t(a, b):
    return lax.dot_general(a, b, (((1,), (1,)), ((), ())), preferred_element_type=F32)


def split2(x):
    hi = x.astype(BF16)
    return hi, (x - hi.astype(F32)).astype(BF16)


def split3(x):
    hi = x.astype(BF16)
    rest = x - hi.astype(F32)
    mid = rest.astype(BF16)
    return hi, mid, (rest - mid.astype(F32)).astype(BF16)


def iota(shape, axis):
    return lax.broadcasted_iota(jnp.int32, shape, axis)


def flag(cond):
    return cond.astype(F32).astype(BF16)


def kernel(
    n_seq, conv_ref, og_ref, k_ref, q_ref, ld_ref, ss_ref, skip_ref, cw_ref,
    igrad_ref, kgrad_ref, qgrad_ref, dgrad_ref, sgrad_ref,
    pad_ld, pad_ss, pad_skip, col_s, row_s, kp, qp, vhi, vlo, vals, dsilu, tsx, whi, wlo, shi, slo, within, wsum,
    lme, lsend, lother, tt, tsend, tlow, uu, dme8, doth8, dchip8, dlow8, xin, xsend, ebuf, epart,
    ext, kpart, qpart, krecv, qrecv,
    kq_ss, kq_rs, d_ss, d_rs, l_ss, l_rs, t_ss, t_rs, x_ss, x2_ss, x_rs, e_ss, e_rs, f_ss, f_rs, c_ss, c_rs,
):
    seq = lax.axis_index("seq")
    head = lax.axis_index("head")
    core = lax.rem(seq, 2)
    chip = seq // 2
    chips = n_seq // 2
    pos = jnp.where(core == 0, chip, chips - 1 - chip)
    group = pos // 2
    high = lax.rem(pos, 2) == 1
    low = lax.rem(pos, 2) == 0
    opens = group == 0
    sends_on = jnp.logical_and(high, group < chips // 2 - 1)
    step1 = jnp.where(core == 0, 2, n_seq - 2)
    step2 = jnp.where(core == 0, 4, n_seq - 4)

    def at(s):
        return (lax.rem(s, n_seq), head)

    next1 = at(seq + step1)
    next2 = at(seq + step2)
    other_core = at(seq + 1 - 2 * core)
    before = at(seq + n_seq - 1)
    after_or_before = at(seq + jnp.where(core == 0, n_seq - 1, 1))
    partner = (seq, head + 1 - 2 * lax.rem(head, 2))

    barrier = pltpu.get_barrier_semaphore()
    greeted = (
        at(seq + 2), at(seq + n_seq - 2), at(seq + 4), at(seq + n_seq - 4), other_core, after_or_before, partner,
    )
    for peer in greeted:
        pl.semaphore_signal(barrier, inc=1, device_id=peer, device_id_type=MESH)

    def remote(src, dst, ss, rs, peer):
        return pltpu.make_async_remote_copy(
            src_ref=src, dst_ref=dst, send_sem=ss, recv_sem=rs, device_id=peer, device_id_type=MESH
        )

    pad_ld[...] = jnp.zeros((LEN, LEN), F32)
    pad_ss[...] = jnp.zeros((LEN, LEN), F32)
    pad_skip[...] = jnp.zeros((8, LEN), F32)
    pad_ld[:, 0:HEADS] = ld_ref[...]
    pad_ss[:, 0:HEADS] = ss_ref[...]
    pad_skip[0:1, 0:HEADS] = skip_ref[...]
    rows = iota((LEN, LEN), 0)
    cols = iota((LEN, LEN), 1)
    lower = flag(rows >= cols)
    spread = flag(iota((LEN, WIDTH), 0) == iota((LEN, WIDTH), 1) // 64)
    gather = flag(iota((WIDTH, LEN), 0) // 64 == iota((WIDTH, LEN), 1))

    def expand(x):
        hi, lo = split2(x)
        return dot(hi, spread) + dot(lo, spread)

    def by_head(x):
        hi, lo = split2(x)
        return dot(hi, gather) + dot(lo, gather)

    hi, mid, lo = split3(pad_ld[...])
    cum = dot(lower, hi) + (dot(lower, mid) + dot(lower, lo))
    step = pad_ss[...]
    from_start = jnp.exp(cum)
    total = cum[LEN - 1 : LEN, :]
    to_end = jnp.exp(total - cum)
    fsx = expand(from_start)
    tsx[...] = expand(to_end * step)
    d_me = fsx[LEN - 1 : LEN, :]
    dme8[...] = jnp.broadcast_to(d_me, (8, WIDTH))

    pl.semaphore_wait(barrier, len(greeted))
    k_copy = remote(k_ref, kp, kq_ss.at[0], kq_rs.at[0], partner)
    q_copy = remote(q_ref, qp, kq_ss.at[1], kq_rs.at[1], partner)
    k_copy.start()
    q_copy.start()
    d_copy = remote(dme8, doth8, d_ss.at[0], d_rs.at[0], other_core)
    d_copy.start()

    preact = conv_ref[...].astype(F32)
    sig = 1.0 / (1.0 + jnp.exp(-preact))
    value = preact * sig
    vals[...] = value
    vhi[...], vlo[...] = split2(value)
    dsilu[...] = sig * (1.0 + preact * (1.0 - sig))
    whi[...], wlo[...] = split2(value * tsx[...])
    shi[...], slo[...] = split2(og_ref[...].astype(F32) * fsx)

    forward = core == 0

    def turned(x):
        return x.astype(F32).T.astype(BF16)

    def local_half(at_row, kk, qq, half):
        kt, qt = turned(kk), turned(qq)
        wh, wl, sh, sl = whi[...], wlo[...], shi[...], slo[...]
        mine, other = jnp.where(forward, kt, qt), jnp.where(forward, qt, kt)
        lsend[at_row : at_row + HALF, :] = dot(other, jnp.where(forward, sh, wh)) + dot(
            other, jnp.where(forward, sl, wl)
        )
        part = pl.ds(at_row, HALF)
        remote(lsend.at[part], lother.at[part], l_ss.at[half], l_rs.at[half], other_core).start()
        lme[at_row : at_row + HALF, :] = dot(mine, jnp.where(forward, wh, sh)) + dot(
            mine, jnp.where(forward, wl, sl)
        )

    local_half(0, k_ref[...], q_ref[...], 0)
    k_copy.wait_recv()
    q_copy.wait_recv()
    local_half(HALF, kp[...], qp[...], 1)

    d_copy.wait_recv()
    d_me8 = dme8[...]
    d_oth8 = doth8[...]
    dchip8[...] = d_me8 * d_oth8

    @pl.when(low)
    def _():
        remote(dchip8, dlow8, d_ss.at[1], d_rs.at[1], next1).start()

    def chip_half(half):
        at_row = half * HALF
        part = pl.ds(at_row, HALF)
        remote(lsend.at[part], lother.at[part], l_ss.at[half], l_rs.at[half], other_core).wait_recv()
        sl = slice(at_row, at_row + HALF)
        whole = d_oth8[0:1, :] * lme[sl, :] + lother[sl, :]
        tt[sl, :] = whole

        @pl.when(low)
        def _():
            tsend[sl, :] = whole
            remote(tsend.at[part], tlow.at[part], t_ss.at[half], t_rs.at[half], next1).start()

    chip_half(0)
    chip_half(1)

    @pl.when(low)
    def _():
        tlow[...] = jnp.zeros((STATE, WIDTH), F32)
        dlow8[...] = jnp.ones((8, WIDTH), F32)

    @pl.when(opens)
    def _():
        xin[...] = jnp.zeros((STATE, WIDTH), F32)

    def group_totals():
        @pl.when(high)
        def _():
            remote(dchip8, dlow8, d_ss.at[1], d_rs.at[1], next1).wait_recv()
            for half in range(2):
                part = pl.ds(half * HALF, HALF)
                sl = slice(half * HALF, half * HALF + HALF)
                remote(tsend.at[part], tlow.at[part], t_ss.at[half], t_rs.at[half], next1).wait_recv()
                uu[sl, :] = dchip8[0:1, :] * tlow[sl, :] + tt[sl, :]

    def x_copy(c, far):
        part = pl.ds(c * CHUNK, CHUNK)
        return remote(
            xsend.at[part], xin.at[part], (x2_ss if far else x_ss).at[c], x_rs.at[c], next2 if far else next1
        )

    def e_copy(c):
        part = pl.ds(c * CHUNK, CHUNK)
        return remote(epart.at[part], ebuf.at[core, part], e_ss.at[c], e_rs.at[c], other_core)

    def chain():
        group_totals()
        a = dlow8[0:1, :]
        dd = dchip8[0:1, :] * a
        dm = dme8[0:1, :]
        for c in range(CHUNKS):
            sl = slice(c * CHUNK, c * CHUNK + CHUNK)

            @pl.when(jnp.logical_not(opens))
            def _():
                x_copy(c, False).wait_recv()

            x = xin[sl, :]

            @pl.when(sends_on)
            def _():
                xsend[sl, :] = dd * x + uu[sl, :]
                x_copy(c, True).start()
                x_copy(c, False).start()

            em = a * x + tlow[sl, :]
            ebuf[core, sl, :] = em
            epart[sl, :] = dm * em + lme[sl, :]
            e_copy(c).start()

    def inside():
        scores = dot_t(k_ref[...], q_ref[...]) + dot_t(kp[...], qp[...])
        causal = rows <= cols
        cum_t = cum.T
        left = iota((LEN, LEN), 1) < 64
        col_s[...] = jnp.zeros((LEN, LEN), F32)
        row_s[...] = jnp.zeros((LEN, LEN), F32)
        weights = jnp.zeros((LEN, LEN), F32)
        for j in range(HEADS // 2):
            lanes = slice(j * 128, j * 128 + 128)
            ogb = og_ref[:, lanes]
            vh, vl = vhi[:, lanes], vlo[:, lanes]
            halves = []
            for e in range(2):
                h = 2 * j + e
                own = left if e == 0 else jnp.logical_not(left)
                none = jnp.zeros_like(vh)
                pd = dot_t(jnp.where(own, vh, none), ogb) + dot_t(jnp.where(own, vl, none), ogb)
                gap = cum_t[h : h + 1, :] - cum[:, h : h + 1]
                dm = jnp.exp(jnp.where(causal, gap, -1e30))
                st = step[:, h : h + 1]
                a = dm * scores
                weights = weights + dm * pd * st
                eff = a * pd
                a_st = a * st
                col_s[:, h : h + 1] = jnp.sum(eff, axis=1, keepdims=True)
                row_s[h : h + 1, :] = jnp.sum(eff * st, axis=0, keepdims=True)
                halves.append(dot(a_st.astype(BF16), ogb))
            within[:, lanes] = jnp.where(left, halves[0], halves[1])
        wsum[...] = weights
        sk_hi, sk_lo = split2(pad_skip[...])
        skip_row = (dot(sk_hi, spread) + dot(sk_lo, spread))[0:1, :]
        within[...] = within[...] + skip_row * og_ref[...].astype(F32)

    def turn(i, carry):
        first = i == 0

        @pl.when(jnp.logical_xor(first, opens))
        def _():
            inside()

        @pl.when(jnp.logical_not(jnp.logical_xor(first, opens)))
        def _():
            chain()

        return carry

    lax.fori_loop(0, 2, turn, 0)

    for c in range(CHUNKS):
        e_copy(c).wait_recv()

    entering = ebuf[0]
    arriving = ebuf[1]
    w = wsum[...]
    wm, wm_t = split2(w), split2(w.T)
    wt = (whi[...], wlo[...])
    sd = (shi[...], slo[...])

    def own_half(x):
        return split2(x[0:HALF, :])

    def far_half(x):
        return split2(x[HALF:, :])

    def twice(a, b):
        return dot(a[0], b) + dot(a[1], b)

    def thrice_t(a, b):
        return dot_t(a[0], b[0]) + (dot_t(a[0], b[1]) + dot_t(a[1], b[0]))

    def left(a, b):
        return dot(a, b[0]) + dot(a, b[1])

    a_far = far_half(arriving)
    kpart[...] = (twice(wm, qp[...]) + thrice_t(wt, a_far)).astype(BF16)
    k_back = remote(kpart, krecv, f_ss.at[0], f_rs.at[0], partner)
    k_back.start()
    e_far = far_half(entering)
    qpart[...] = (twice(wm_t, kp[...]) + thrice_t(sd, e_far)).astype(BF16)
    q_back = remote(qpart, qrecv, f_ss.at[1], f_rs.at[1], partner)
    q_back.start()

    a_own, e_own = own_half(arriving), own_half(entering)
    into = left(k_ref[...], a_own) + left(kp[...], a_far)
    ext[0:LEN, :] = (within[...] + tsx[...] * into) * dsilu[...]
    c_copy = remote(ext.at[pl.ds(0, 8)], ext.at[pl.ds(LEN, 8)], c_ss.at[0], c_rs.at[0], before)

    @pl.when(seq > 0)
    def _():
        c_copy.start()

    @pl.when(seq == n_seq - 1)
    def _():
        ext[LEN : LEN + 8, :] = jnp.zeros((8, WIDTH), F32)

    k_own = twice(wm, q_ref[...]) + thrice_t(wt, a_own)
    q_own = twice(wm_t, k_ref[...]) + thrice_t(sd, e_own)
    out_of = left(q_ref[...], e_own) + left(qp[...], e_far)
    carried = by_head(vals[...] * into)
    read = by_head(og_ref[...].astype(F32) * out_of)
    cross = jnp.sum(entering * arriving, axis=0, keepdims=True)
    cross = by_head(jnp.broadcast_to(cross, (8, WIDTH)))[0:1, :]
    col = col_s[...]
    row = row_s[...].T
    sgrad_ref[...] = (col + to_end * carried)[:, 0:HEADS]
    later = row - col * step + from_start * read
    earlier = to_end * step * carried
    upper = flag(rows <= cols)
    strict = flag(rows > cols)
    lh, ll = split2(later)
    eh, el = split2(earlier)
    decay = dot(upper, lh) + dot(upper, ll) + dot(strict, eh) + dot(strict, el)
    decay = decay + jnp.exp(total) * cross
    dgrad_ref[...] = decay[:, 0:HEADS]

    k_back.wait_recv()
    kgrad_ref[...] = k_own + krecv[...].astype(F32)
    q_back.wait_recv()
    qgrad_ref[...] = q_own + qrecv[...].astype(F32)

    @pl.when(seq < n_seq - 1)
    def _():
        c_copy.wait_recv()

    acc = cw_ref[3:4, :] * ext[0:LEN, :]
    for tap in range(3):
        acc = acc + cw_ref[tap : tap + 1, :] * ext[3 - tap : 3 - tap + LEN, :]
    igrad_ref[...] = acc.astype(BF16)

    k_copy.wait_send()
    q_copy.wait_send()
    d_copy.wait_send()
    for half in range(2):
        part = pl.ds(half * HALF, HALF)
        remote(lsend.at[part], lother.at[part], l_ss.at[half], l_rs.at[half], other_core).wait_send()

    @pl.when(low)
    def _():
        remote(dchip8, dlow8, d_ss.at[1], d_rs.at[1], next1).wait_send()
        for half in range(2):
            part = pl.ds(half * HALF, HALF)
            remote(tsend.at[part], tlow.at[part], t_ss.at[half], t_rs.at[half], next1).wait_send()

    @pl.when(sends_on)
    def _():
        for c in range(CHUNKS):
            x_copy(c, True).wait_send()
            x_copy(c, False).wait_send()

    for c in range(CHUNKS):
        e_copy(c).wait_send()
    k_back.wait_send()
    q_back.wait_send()

    @pl.when(seq > 0)
    def _():
        c_copy.wait_send()


def body(n_seq, conv_output, output_grad, write_keys, read_queries, log_decay, step_size, skip_gain, conv_weight):
    shape = jax.ShapeDtypeStruct
    vmem = pltpu.VMEM
    dma = pltpu.SemaphoreType.DMA
    big = (STATE, WIDTH)
    tok = (LEN, WIDTH)
    sq = (LEN, LEN)
    return pl.pallas_call(
        functools.partial(kernel, n_seq),
        out_shape=(
            shape(tok, BF16), shape(sq, F32), shape(sq, F32), shape((LEN, HEADS), F32), shape((LEN, HEADS), F32),
        ),
        in_specs=[pl.BlockSpec(memory_space=vmem)] * 8,
        out_specs=(pl.BlockSpec(memory_space=vmem),) * 5,
        scratch_shapes=[
            vmem(sq, F32), vmem(sq, F32), vmem((8, LEN), F32), vmem(sq, F32), vmem(sq, F32),
            vmem(sq, BF16), vmem(sq, BF16), vmem(tok, BF16), vmem(tok, BF16), vmem(tok, F32), vmem(tok, F32),
            vmem(tok, F32), vmem(tok, BF16), vmem(tok, BF16), vmem(tok, BF16), vmem(tok, BF16),
            vmem(tok, F32), vmem(sq, F32),
            vmem(big, F32), vmem(big, F32), vmem(big, F32),
            vmem(big, F32), vmem(big, F32), vmem(big, F32), vmem(big, F32),
            vmem((8, WIDTH), F32), vmem((8, WIDTH), F32), vmem((8, WIDTH), F32), vmem((8, WIDTH), F32),
            vmem(big, F32), vmem(big, F32), vmem((2,) + big, F32), vmem(big, F32),
            vmem((LEN + 8, WIDTH), F32), vmem(sq, BF16), vmem(sq, BF16), vmem(sq, BF16), vmem(sq, BF16),
            dma((2,)), dma((2,)), dma((2,)), dma((2,)), dma((2,)), dma((2,)), dma((2,)), dma((2,)),
            dma((CHUNKS,)), dma((CHUNKS,)), dma((CHUNKS,)), dma((CHUNKS,)), dma((CHUNKS,)),
            dma((2,)), dma((2,)), dma((1,)), dma((1,)),
        ],
        compiler_params=pltpu.CompilerParams(
            collective_id=0, has_side_effects=True, vmem_limit_bytes=40 * 1024 * 1024
        ),
        cost_estimate=pl.CostEstimate(flops=300_000_000, bytes_accessed=1_000_000, transcendentals=300_000),
    )(
        conv_output, output_grad, write_keys, read_queries, log_decay, step_size,
        skip_gain.reshape(1, HEADS), conv_weight,
    )


def solution(mesh):
    spec = P("seq", "head")
    return jax.shard_map(
        functools.partial(body, mesh.shape["seq"]),
        mesh=mesh,
        in_specs=(spec, spec, spec, spec, spec, spec, P("head"), P(None, "head")),
        out_specs=(spec,) * 5,
        check_vma=False,
    )
```

time: 400 us -> 66.9 us (0.17); the launches traced: 395 us -> 66.6 us
  waiting for transfers between devices: 154 us -> 0 us
  local copies, waits for them, and re-layouts: 125 us -> 7.28 us
  Pallas kernels: 0 us -> 58.6 us
  blocking collectives: 37.4 us -> 0 us
  other arithmetic: 30.5 us -> 0 us
  matrix products: 16 us -> 0 us
  starting transfers between devices: 14.4 us -> 0 us
  between operations: 14.5 us -> 0.69 us
    all_gather x2 -> x0, waiting for transfers between devices: 154 us -> none  [carried_in(): everything = jax.tree.map(lambda part: lax.all_gather(part, axis), shard)]
    dynamic_slice x128 -> x0, local copies, waits for them, and re-layouts: 90.7 us -> none  [lap(): new = combine(before, jax.tree.map(lambda part: part[at], everything))]
    pallas_call x0 -> x1, Pallas kernels: none -> 58.6 us  [body(): pl.pallas_call(functools.partial(kernel, n_seq), out_shape=(shape(tok, BF...]
    all_gather x1 -> x0, blocking collectives: 37.4 us -> none  [carried_in(): everything = jax.tree.map(lambda part: lax.all_gather(part, axis), shard)]
    mul x66 -> x0, local copies, waits for them, and re-layouts: 22.5 us -> none  [the longest x32 22 us: forward_combine(): latter[0][:, None, None] * earlier[1] + latter[1]]
    select_n x64 -> x0, other arithmetic: 22.5 us -> none  [lap(): return jax.tree.map(lambda a, b: jnp.where(reached, a, b), new, before)]
    dot_general x10 -> x0, matrix products: 14.4 us -> none  [the longest x2 2.06 us: product(): jnp.dot(left, right, preferred_element_type=jnp.float32, precision=precise)]
    ppermute x5 -> x0, starting transfers between devices: 14.3 us -> none  [the longest x4 12.2 us: swapped(): return lax.ppermute(block, axis, route)]
  transfers between devices with their start and end apart: 7 -> 0, of which waited for: 2 -> 0; matrix products, arithmetic and copies ran while one was open for 6% -> 0% of each run, Pallas kernels for 0% -> 0%
where the time goes in v1:
time: 66.9 us; the launch traced here: 66.6 us
  Pallas kernels  58.6 us (88%)
  local copies, waits for them, and re-layouts  7.28 us (11%)
  between operations  0.69 us (1%)
    pallas_call x1, Pallas kernels, body(): pl.pallas_call(functools.partial(kernel, n_seq), out_shape=(shape(tok, BF...  58.6 us
    unnamed x17, local copies, waits for them, and re-layouts  5.96 us

profile of v1, /device:TPU:1, one launch (start us, length us, event | category | flops | bytes accessed | tf_op | source)
XLA Modules:
  0.0 66.6 jit_solution(1287094548858082417)
XLA Ops:
  0.6 0.0 copy-start
  0.6 0.8 %copy.13.ld_ref = f32[128,8]{1,0:T(8,128)S(1)} copy(f32[128,8]{0,1:T(8,128)} %param.12) | data formatting | bytes 8192 | tf_op args[4]
  1.5 0.0 copy-start.4
  1.5 0.0 copy-start.5
  1.5 0.8 %copy.14.ss_ref = f32[128,8]{1,0:T(8,128)S(1)} copy(f32[128,8]{0,1:T(8,128)} %param.13) | data formatting | bytes 8192 | tf_op args[5]
  2.3 0.0 copy-done
  2.3 0.0 copy-done.4
  2.3 0.0 copy-done.5
  2.3 0.0 copy-start.1
  2.3 0.9 %copy-done.1 = bf16[128,512]{1,0:T(8,128)(2,1)S(1)} copy-done((bf16[128,512]{1,0:T(8,128)(2,1)S(1)}, bf16[128,512]{1,0:T(8,128)(2,1)}, u32[]{:S(2)}) %copy-start.1) | copy-done | bytes 131096
  3.2 0.0 copy-start.2
  3.2 0.8 %copy-done.2 = bf16[128,128]{1,0:T(8,128)(2,1)S(1)} copy-done((bf16[128,128]{1,0:T(8,128)(2,1)S(1)}, bf16[128,128]{1,0:T(8,128)(2,1)}, u32[]{:S(2)}) %copy-start.2) | copy-done | bytes 32792
  4.0 0.0 copy-start.3
  4.0 0.8 %copy-done.3 = bf16[128,128]{1,0:T(8,128)(2,1)S(1)} copy-done((bf16[128,128]{1,0:T(8,128)(2,1)S(1)}, bf16[128,128]{1,0:T(8,128)(2,1)}, u32[]{:S(2)}) %copy-start.3) | copy-done | bytes 32792
  4.7 58.6 %shard_map.119 = (bf16[128,512]{1,0:T(8,128)(2,1)S(1)}, f32[128,128]{1,0:T(8,128)S(1)}, f32[128,128]{1,0:T(8,128)S(1)}, f32[128,8]{1,0:T(8,128)S(1)}, f32[128,8]{1,0:T(8,128)S(1)}) custom-call(bf16[128,512]{1,0:T(8,128)(2,1)S(1)} %copy-done, bf16[128,512]{1,0:T(8,128)(2,1)S(1)} %copy-done.1, bf16[128,128]{1,0:T(8,128)(2,1)S(1)} %copy-done.2, ...), custom_call_target="tpu_custom_call" | custom-call | flops 300000000 | bytes 1000000 | tf_op jit(solution)/shard_map/pallas_call | solution.py:411
  63.4 0.7 copy.15
  64.0 0.7 copy.16
  64.7 0.7 copy.20
  65.3 0.6 copy.21
  66.0 0.6 copy.22
Async XLA Ops:
  0.6 1.7 %copy-start = (bf16[128,512]{1,0:T(8,128)(2,1)S(1)}, bf16[128,512]{1,0:T(8,128)(2,1)}, u32[]{:S(2)}) copy-start(bf16[128,512]{1,0:T(8,128)(2,1)} %conv_ref.1) | copy-start | bytes 393220
  1.5 0.8 %copy-start.4 = (f32[4,512]{1,0:T(4,128)S(1)}, f32[4,512]{1,0:T(4,128)}, u32[]{:S(2)}) copy-start(f32[4,512]{1,0:T(4,128)} %cw_ref.1) | copy-start | bytes 24580
  1.5 0.8 %copy-start.5 = (f32[8]{0:T(128)S(1)}, f32[8]{0:T(128)}, u32[]{:S(2)}) copy-start(f32[8]{0:T(128)} %param.14) | copy-start | bytes 100
  2.3 0.9 %copy-start.1 = (bf16[128,512]{1,0:T(8,128)(2,1)S(1)}, bf16[128,512]{1,0:T(8,128)(2,1)}, u32[]{:S(2)}) copy-start(bf16[128,512]{1,0:T(8,128)(2,1)} %og_ref.1) | copy-start | bytes 393220
  3.2 0.8 %copy-start.2 = (bf16[128,128]{1,0:T(8,128)(2,1)S(1)}, bf16[128,128]{1,0:T(8,128)(2,1)}, u32[]{:S(2)}) copy-start(bf16[128,128]{1,0:T(8,128)(2,1)} %k_ref.1) | copy-start | bytes 98308
  4.0 0.8 %copy-start.3 = (bf16[128,128]{1,0:T(8,128)(2,1)S(1)}, bf16[128,128]{1,0:T(8,128)(2,1)}, u32[]{:S(2)}) copy-start(bf16[128,128]{1,0:T(8,128)(2,1)} %q_ref.1) | copy-start | bytes 98308

commit v2 on v1

v2 whole, which is shorter than its diff:
```python
import functools

import jax
import jax.numpy as jnp
from jax import lax
from jax.experimental import pallas as pl
from jax.experimental.pallas import tpu as pltpu
from jax.sharding import PartitionSpec as P

MESH = pl.DeviceIdType.MESH
F32 = jnp.float32
BF16 = jnp.bfloat16
LEN = 128
WIDTH = 512
HEADS = 8
HALF = 128
VMEM_BYTES = 58000 * 1024
STATE = 256
CHUNK = 16
CHUNKS = STATE // CHUNK
NEAR_LAG = 1


def dot(a, b):
    return lax.dot_general(a, b, (((1,), (0,)), ((), ())), preferred_element_type=F32)


def dot_t(a, b):
    return lax.dot_general(a, b, (((1,), (1,)), ((), ())), preferred_element_type=F32)


def split2(x):
    hi = x.astype(BF16)
    return hi, (x - hi.astype(F32)).astype(BF16)


def split3(x):
    hi = x.astype(BF16)
    rest = x - hi.astype(F32)
    mid = rest.astype(BF16)
    return hi, mid, (rest - mid.astype(F32)).astype(BF16)


def iota(shape, axis):
    return lax.broadcasted_iota(jnp.int32, shape, axis)


def flag(cond):
    return cond.astype(F32).astype(BF16)


def kernel(
    n_seq, conv_hbm, og_hbm, k_hbm, q_hbm, ld_hbm, ss_hbm, skip_hbm, cw_hbm,
    igrad_ref, kgrad_ref, qgrad_ref, dgrad_ref, sgrad_ref,
    conv_ref, og_ref, k_ref, q_ref, ld_ref, ss_ref, skip_ref, cw_ref,
    pack, col_s, row_s, kp, qp, vhi, vlo, vals, dsilu, tsx, whi, wlo, shi, slo, within,
    k_in, q_in, k_far, q_far, read_s, carried_s,
    lme, lsend, lother, tt, tlow, dme8, doth8, dchip8, dlow8, xin, xsend, xnear, xnsend, ebuf, epart,
    ext, kpart, qpart, krecv, qrecv,
    in_s, kq_ss, kq_rs, d_ss, d_rs, l_ss, l_rs, t_ss, t_rs, x_ss, x2_ss, x_rs, n_rs, e_ss, e_rs, f_ss, f_rs, c_ss, c_rs,
):
    seq = lax.axis_index("seq")
    head = lax.axis_index("head")
    core = lax.rem(seq, 2)
    chip = seq // 2
    chips = n_seq // 2
    pos = jnp.where(core == 0, chip, chips - 1 - chip)
    group = pos // 2
    high = lax.rem(pos, 2) == 1
    low = lax.rem(pos, 2) == 0
    opens = group == 0
    late = group >= chips // 4
    sends_on = jnp.logical_and(high, group < chips // 2 - 1)
    step1 = jnp.where(core == 0, 2, n_seq - 2)
    step2 = jnp.where(core == 0, 4, n_seq - 4)

    def at(s):
        return (lax.rem(s, n_seq), head)

    next1 = at(seq + step1)
    next2 = at(seq + step2)
    other_core = at(seq + 1 - 2 * core)
    before = at(seq + n_seq - 1)
    after_or_before = at(seq + jnp.where(core == 0, n_seq - 1, 1))
    partner = (seq, head + 1 - 2 * lax.rem(head, 2))

    barrier = pltpu.get_barrier_semaphore()
    greeted = (
        at(seq + 2), at(seq + n_seq - 2), at(seq + 4), at(seq + n_seq - 4), other_core, after_or_before, partner,
    )
    for peer in greeted:
        pl.semaphore_signal(barrier, inc=1, device_id=peer, device_id_type=MESH)

    moves = [
        pltpu.make_async_copy(src, dst, in_s.at[n])
        for n, (src, dst) in enumerate((
            (ld_hbm, ld_ref), (ss_hbm, ss_ref), (conv_hbm, conv_ref), (og_hbm, og_ref),
            (k_hbm, k_ref), (q_hbm, q_ref), (skip_hbm, skip_ref), (cw_hbm, cw_ref),
        ))
    ]
    for move in moves:
        move.start()

    def remote(src, dst, ss, rs, peer):
        return pltpu.make_async_remote_copy(
            src_ref=src, dst_ref=dst, send_sem=ss, recv_sem=rs, device_id=peer, device_id_type=MESH
        )

    rows = iota((LEN, LEN), 0)
    cols = iota((LEN, LEN), 1)
    upto = flag(rows <= cols)
    pack[...] = jnp.zeros((LEN, LEN), F32)
    heads_rows = flag(iota((HEADS, WIDTH), 0) == iota((HEADS, WIDTH), 1) // 64)

    def spread(base):
        return flag(iota((LEN, WIDTH), 0) - base == iota((LEN, WIDTH), 1) // 64)

    def by_head(x):
        hi, lo = split2(x)
        return dot_t(heads_rows, hi) + dot_t(heads_rows, lo)

    moves[0].wait()
    moves[1].wait()
    hi, mid, lo = split3(ld_ref[...])
    cum_t = dot(hi, upto) + (dot(mid, upto) + dot(lo, upto))
    step_t = ss_ref[...]
    total = cum_t[:, LEN - 1 : LEN]
    from_start = jnp.exp(cum_t)
    to_end = jnp.exp(total - cum_t)
    pack[0:8, :] = cum_t
    pack[8:16, :] = step_t
    pack[16:24, :] = from_start
    pack[24:32, :] = to_end * step_t
    columns = pack[...].T
    c_hi, c_lo = split2(columns)
    fs_sel, ts_sel = spread(16), spread(24)
    fsx = dot(c_hi, fs_sel) + dot(c_lo, fs_sel)
    tsx[...] = dot(c_hi, ts_sel) + dot(c_lo, ts_sel)
    dme8[...] = jnp.broadcast_to(fsx[LEN - 1 : LEN, :], (8, WIDTH))

    pl.semaphore_wait(barrier, len(greeted))
    k_copy = remote(k_hbm, kp, kq_ss.at[0], kq_rs.at[0], partner)
    q_copy = remote(q_hbm, qp, kq_ss.at[1], kq_rs.at[1], partner)
    k_copy.start()
    q_copy.start()
    d_copy = remote(dme8, doth8, d_ss.at[0], d_rs.at[0], other_core)
    d_copy.start()

    moves[2].wait()
    preact = conv_ref[...].astype(F32)
    sig = 1.0 / (1.0 + jnp.exp(-preact))
    value = preact * sig
    vals[...] = value
    vhi[...], vlo[...] = split2(value)
    dsilu[...] = sig * (1.0 + preact * (1.0 - sig))
    whi[...], wlo[...] = split2(value * tsx[...])
    moves[3].wait()
    shi[...], slo[...] = split2(og_ref[...].astype(F32) * fsx)

    forward = core == 0

    def turned(x):
        return x.astype(F32).T.astype(BF16)

    def l_copy(half):
        part = pl.ds(half * HALF, HALF)
        return remote(lsend.at[part], lother.at[part], l_ss.at[half], l_rs.at[half], other_core)

    def local_half(half, kk, qq):
        sl = slice(half * HALF, half * HALF + HALF)
        kt, qt = turned(kk), turned(qq)
        wh, wl, sh, slw = whi[...], wlo[...], shi[...], slo[...]
        mine, other = jnp.where(forward, kt, qt), jnp.where(forward, qt, kt)
        lsend[sl, :] = dot(other, jnp.where(forward, sh, wh)) + dot(other, jnp.where(forward, slw, wl))
        l_copy(half).start()
        lme[sl, :] = dot(mine, jnp.where(forward, wh, sh)) + dot(mine, jnp.where(forward, wl, slw))

    moves[4].wait()
    moves[5].wait()
    local_half(0, k_ref[...], q_ref[...])
    k_copy.wait_recv()
    q_copy.wait_recv()
    local_half(1, kp[...], qp[...])
    moves[6].wait()
    moves[7].wait()

    d_copy.wait_recv()
    dchip8[...] = dme8[...] * doth8[...]

    def dt_copy():
        return remote(dchip8, dlow8, d_ss.at[1], d_rs.at[1], next1)

    def t_copy(c):
        part = pl.ds(c * CHUNK, CHUNK)
        return remote(tt.at[part], tlow.at[part], t_ss.at[c], t_rs.at[c], next1)

    @pl.when(low)
    def _():
        dt_copy().start()

    for c in range(CHUNKS):
        sl = slice(c * CHUNK, c * CHUNK + CHUNK)
        if c % (CHUNKS // 2) == 0:
            l_copy(c // (CHUNKS // 2)).wait_recv()
        tt[sl, :] = doth8[0:1, :] * lme[sl, :] + lother[sl, :]

        @pl.when(low)
        def _():
            t_copy(c).start()

    @pl.when(low)
    def _():
        tlow[...] = jnp.zeros((STATE, WIDTH), F32)
        dlow8[...] = jnp.ones((8, WIDTH), F32)

    @pl.when(opens)
    def _():
        xin[...] = jnp.zeros((STATE, WIDTH), F32)

    def x_copy(c, far):
        part = pl.ds(c * CHUNK, CHUNK)
        if far:
            return remote(xsend.at[part], xin.at[part], x2_ss.at[c], x_rs.at[c], next2)
        return remote(xnsend.at[part], xnear.at[part], x_ss.at[c], n_rs.at[c], next1)

    def e_copy(c):
        part = pl.ds(c * CHUNK, CHUNK)
        return remote(epart.at[part], ebuf.at[core, part], e_ss.at[c], e_rs.at[c], other_core)

    def chain():
        @pl.when(high)
        def _():
            dt_copy().wait_recv()

        a = dlow8[0:1, :]
        dchip = dchip8[0:1, :]
        dd = dchip * a
        dm = dme8[0:1, :]
        def forward_chunk(c):
            sl = slice(c * CHUNK, c * CHUNK + CHUNK)

            @pl.when(high)
            def _():
                t_copy(c).wait_recv()

            @pl.when(jnp.logical_and(high, jnp.logical_not(opens)))
            def _():
                x_copy(c, True).wait_recv()

            @pl.when(jnp.logical_and(low, jnp.logical_not(opens)))
            def _():
                x_copy(c, False).wait_recv()
                xin[sl, :] = xnear[sl, :].astype(F32)

            @pl.when(sends_on)
            def _():
                xsend[sl, :] = dd * xin[sl, :] + (dchip * tlow[sl, :] + tt[sl, :])
                x_copy(c, True).start()
                xnsend[sl, :] = xsend[sl, :].astype(BF16)

        def use_chunk(c):
            sl = slice(c * CHUNK, c * CHUNK + CHUNK)
            em = a * xin[sl, :] + tlow[sl, :]
            ebuf[core, sl, :] = em
            epart[sl, :] = dm * em + lme[sl, :]
            e_copy(c).start()

        for c in range(CHUNKS + NEAR_LAG):
            if c < CHUNKS:
                forward_chunk(c)
            if c >= NEAR_LAG:
                pl.when(sends_on)(x_copy(c - NEAR_LAG, False).start)
            if 1 <= c <= CHUNKS:
                use_chunk(c - 1)

    def inside():
        scores = dot_t(k_ref[...], q_ref[...]) + dot_t(kp[...], qp[...])
        causal = rows <= cols
        left = iota((LEN, LEN), 1) < 64
        col_s[...] = jnp.zeros((LEN, LEN), F32)
        weights = jnp.zeros((LEN, LEN), F32)
        for j in range(HEADS // 2):
            lanes = slice(j * 128, j * 128 + 128)
            ogb = og_ref[:, lanes]
            vh, vl = vhi[:, lanes], vlo[:, lanes]
            none = jnp.zeros_like(vh)
            halves = []
            for e in range(2):
                h = 2 * j + e
                own = left if e == 0 else jnp.logical_not(left)
                pd = dot_t(jnp.where(own, vh, none), ogb) + dot_t(jnp.where(own, vl, none), ogb)
                gap = cum_t[h : h + 1, :] - columns[:, h : h + 1]
                dm = jnp.exp(jnp.where(causal, gap, -1e30))
                st = columns[:, 8 + h : 9 + h]
                dm_st = dm * st
                weights = weights + dm_st * pd
                eff = dm * scores * pd
                col_s[:, h : h + 1] = jnp.sum(eff, axis=1, keepdims=True)
                row_s[h : h + 1, :] = jnp.sum(eff * st, axis=0, keepdims=True)
                halves.append(dot((dm_st * scores).astype(BF16), ogb))
            within[:, lanes] = jnp.where(left, halves[0], halves[1])
        w16 = weights.astype(BF16)
        w16_t = weights.T.astype(BF16)
        k_far[...] = dot(w16, qp[...])
        q_far[...] = dot(w16_t, kp[...])
        k_in[...] = dot(w16, q_ref[...])
        q_in[...] = dot(w16_t, k_ref[...])
        skips = jnp.broadcast_to(skip_ref[...], (LEN, HEADS))
        sk_hi, sk_lo = split2(skips)
        skip_row = (dot(sk_hi, heads_rows) + dot(sk_lo, heads_rows))[0:1, :]
        within[...] = within[...] + skip_row * og_ref[...].astype(F32)

    k_back = remote(kpart, krecv, f_ss.at[0], f_rs.at[0], partner)
    q_back = remote(qpart, qrecv, f_ss.at[1], f_rs.at[1], partner)
    c_copy = remote(ext.at[pl.ds(0, 8)], ext.at[pl.ds(LEN, 8)], c_ss.at[0], c_rs.at[0], before)

    def both(a, b):
        return dot(a, b[0]) + dot(a, b[1])

    def with_entering():
        @pl.when(core == 1)
        def _():
            for c in range(CHUNKS):
                e_copy(c).wait_recv()

        far = split2(ebuf[0, HALF:, :])
        qpart[...] = (q_far[...] + dot_t(shi[...], far[0])).astype(BF16)
        q_back.start()
        own = split2(ebuf[0, 0:HALF, :])
        out_of = both(q_ref[...], own) + both(qp[...], far)
        read_s[...] = by_head(og_ref[...].astype(F32) * out_of)
        q_in[...] = q_in[...] + dot_t(shi[...], own[0])

    def with_arriving():
        @pl.when(core == 0)
        def _():
            for c in range(CHUNKS):
                e_copy(c).wait_recv()

        far = split2(ebuf[1, HALF:, :])
        kpart[...] = (k_far[...] + dot_t(whi[...], far[0])).astype(BF16)
        k_back.start()
        own = split2(ebuf[1, 0:HALF, :])
        into = both(k_ref[...], own) + both(kp[...], far)
        ext[0:LEN, :] = (within[...] + tsx[...] * into) * dsilu[...]

        @pl.when(seq > 0)
        def _():
            c_copy.start()

        carried_s[...] = by_head(vals[...] * into)
        k_in[...] = k_in[...] + dot_t(whi[...], own[0])

    mine = jnp.where(forward, 2, 3)
    theirs = 5 - mine

    def turn(i, carry):
        early = jnp.where(i < 2, jnp.where(jnp.logical_xor(i == 0, opens), 1, 0), jnp.where(i == 2, mine, theirs))
        later = jnp.where(i == 0, 1, jnp.where(i == 1, theirs, jnp.where(i == 2, 0, mine)))
        what = jnp.where(late, later, early)
        for n, part in enumerate((chain, inside, with_entering, with_arriving)):
            pl.when(what == n)(part)
        return carry

    lax.fori_loop(0, 4, turn, 0)

    @pl.when(seq == n_seq - 1)
    def _():
        ext[LEN : LEN + 8, :] = jnp.zeros((8, WIDTH), F32)

    cross = jnp.sum(ebuf[0] * ebuf[1], axis=0, keepdims=True)
    cross = by_head(jnp.broadcast_to(cross, (8, WIDTH)))[:, 0:1]
    col = col_s[...].T[0:HEADS, :]
    carried = carried_s[...]
    sgrad_ref[...] = col + to_end * carried
    lh, ll = split2(row_s[...] - col * step_t + from_start * read_s[...])
    eh, el = split2(to_end * step_t * carried)
    since = flag(rows >= cols)
    strict = flag(rows < cols)
    decay = dot(lh, since) + dot(ll, since) + dot(eh, strict) + dot(el, strict)
    dgrad_ref[...] = decay + jnp.exp(total) * cross

    @pl.when(seq < n_seq - 1)
    def _():
        c_copy.wait_recv()

    acc = cw_ref[3:4, :] * ext[0:LEN, :]
    for tap in range(3):
        acc = acc + cw_ref[tap : tap + 1, :] * ext[3 - tap : 3 - tap + LEN, :]
    igrad_ref[...] = acc.astype(BF16)

    k_back.wait_recv()
    kgrad_ref[...] = k_in[...] + krecv[...].astype(F32)
    q_back.wait_recv()
    qgrad_ref[...] = q_in[...] + qrecv[...].astype(F32)

    k_copy.wait_send()
    q_copy.wait_send()
    d_copy.wait_send()
    for half in range(2):
        l_copy(half).wait_send()

    @pl.when(low)
    def _():
        dt_copy().wait_send()
        for c in range(CHUNKS):
            t_copy(c).wait_send()

    @pl.when(sends_on)
    def _():
        for c in range(CHUNKS):
            x_copy(c, True).wait_send()
            x_copy(c, False).wait_send()

    for c in range(CHUNKS):
        e_copy(c).wait_send()
    k_back.wait_send()
    q_back.wait_send()

    @pl.when(seq > 0)
    def _():
        c_copy.wait_send()


def store_kernel(*refs):
    sems = refs[-1]
    moves = [pltpu.make_async_copy(refs[n], refs[n + 5], sems.at[n]) for n in range(5)]
    for move in moves:
        move.start()
    for move in moves:
        move.wait()


def body(n_seq, conv_output, output_grad, write_keys, read_queries, log_decay, step_size, skip_gain, conv_weight):
    shape = jax.ShapeDtypeStruct
    vmem = pltpu.VMEM
    dma = pltpu.SemaphoreType.DMA
    big = (STATE, WIDTH)
    tok = (LEN, WIDTH)
    sq = (LEN, LEN)
    small = (HEADS, LEN)
    row = (8, WIDTH)
    in_vmem = pl.BlockSpec(memory_space=vmem)
    hbm = pl.BlockSpec(memory_space=pltpu.HBM)
    outs = (shape(tok, BF16), shape(sq, F32), shape(sq, F32), shape(small, F32), shape(small, F32))
    results = pl.pallas_call(
        functools.partial(kernel, n_seq),
        out_shape=tuple(vmem(o.shape, o.dtype) for o in outs),
        in_specs=[hbm] * 8,
        out_specs=(in_vmem,) * 5,
        scratch_shapes=[
            vmem(tok, BF16), vmem(tok, BF16), vmem(sq, BF16), vmem(sq, BF16),
            vmem(small, F32), vmem(small, F32), vmem((1, HEADS), F32), vmem((4, WIDTH), F32),
            vmem(sq, F32), vmem(sq, F32), vmem(small, F32), vmem(sq, BF16), vmem(sq, BF16),
            vmem(tok, BF16), vmem(tok, BF16), vmem(tok, F32), vmem(tok, F32), vmem(tok, F32),
            vmem(tok, BF16), vmem(tok, BF16), vmem(tok, BF16), vmem(tok, BF16), vmem(tok, F32),
            vmem(sq, F32), vmem(sq, F32), vmem(sq, F32), vmem(sq, F32), vmem(small, F32), vmem(small, F32),
            vmem(big, F32), vmem(big, F32), vmem(big, F32),
            vmem(big, F32), vmem(big, F32),
            vmem(row, F32), vmem(row, F32), vmem(row, F32), vmem(row, F32),
            vmem(big, F32), vmem(big, F32), vmem(big, BF16), vmem(big, BF16), vmem((2,) + big, F32), vmem(big, F32),
            vmem((LEN + 8, WIDTH), F32), vmem(sq, BF16), vmem(sq, BF16), vmem(sq, BF16), vmem(sq, BF16),
            dma((8,)), dma((2,)), dma((2,)), dma((2,)), dma((2,)), dma((2,)), dma((2,)),
            dma((CHUNKS,)), dma((CHUNKS,)),
            dma((CHUNKS,)), dma((CHUNKS,)), dma((CHUNKS,)), dma((CHUNKS,)), dma((CHUNKS,)), dma((CHUNKS,)),
            dma((2,)), dma((2,)), dma((1,)), dma((1,)),
        ],
        compiler_params=pltpu.CompilerParams(
            collective_id=0, has_side_effects=True, vmem_limit_bytes=VMEM_BYTES
        ),
        cost_estimate=pl.CostEstimate(flops=300_000_000, bytes_accessed=1_000_000, transcendentals=300_000),
    )(
        conv_output, output_grad, write_keys, read_queries, log_decay.T, step_size.T,
        skip_gain.reshape(1, HEADS), conv_weight,
    )
    igrad, kgrad, qgrad, dgrad, sgrad = pl.pallas_call(
        store_kernel,
        out_shape=outs,
        in_specs=[pl.BlockSpec(memory_space=pl.ANY)] * 5,
        out_specs=(hbm,) * 5,
        scratch_shapes=[dma((5,))],
        compiler_params=pltpu.CompilerParams(vmem_limit_bytes=16 * 1024 * 1024),
    )(*results)
    return igrad, kgrad, qgrad, dgrad.T, sgrad.T


def solution(mesh):
    spec = P("seq", "head")
    return jax.shard_map(
        functools.partial(body, mesh.shape["seq"]),
        mesh=mesh,
        in_specs=(spec, spec, spec, spec, spec, spec, P("head"), P(None, "head")),
        out_specs=(spec,) * 5,
        check_vma=False,
    )
```

time: 66.9 us -> 62.3 us (0.931)
  local copies, waits for them, and re-layouts: 7.28 us -> 0 us
  Pallas kernels: 58.6 us -> 61.5 us
    unnamed x17 -> x0, local copies, waits for them, and re-layouts: 5.96 us -> none
    pallas_call x1 -> x2, Pallas kernels: 58.6 us -> 61.5 us  [the longest x1 60.7 us: body(): pl.pallas_call(functools.partial(kernel, n_seq), out_shape=tuple((vmem(o....]
    pallas_call x2 -> x0, local copies, waits for them, and re-layouts: 1.32 us -> none  [body(): pl.pallas_call(functools.partial(kernel, n_seq), out_shape=(shape(tok, BF...]
where the time goes in v2:
time: 62.3 us; the launch traced here: 62.1 us
  Pallas kernels  61.5 us (99%)
  between operations  0.64 us (1%)
    pallas_call x1, Pallas kernels, body(): pl.pallas_call(functools.partial(kernel, n_seq), out_shape=tuple((vmem(o....  60.7 us

profile of v2, /device:TPU:1, one launch (start us, length us, event | category | flops | bytes accessed | tf_op | source)
XLA Modules:
  0.0 62.1 jit_solution(5476712594002989793)
XLA Ops:
  0.6 60.7 %shard_map.119 = (bf16[128,512]{1,0:T(8,128)(2,1)S(1)}, f32[128,128]{1,0:T(8,128)S(1)}, f32[128,128]{1,0:T(8,128)S(1)}, f32[8,128]{1,0:T(8,128)S(1)}, f32[8,128]{1,0:T(8,128)S(1)}) custom-call(bf16[128,512]{1,0:T(8,128)(2,1)} %conv_hbm.1, bf16[128,512]{1,0:T(8,128)(2,1)} %og_hbm.1, bf16[128,128]{1,0:T(8,128)(2,1)} %k_hbm.1, bf16[128,128]{1,0:T(8,128)(2,1)} %q_hbm.1, ...), custom_call_target="tpu_custom_call" | custom-call | flops 300000000 | bytes 1000000 | tf_op jit(solution)/shard_map/pallas_call | solution.py:446
  61.4 0.7 %shard_map.120 = (bf16[128,512]{1,0:T(8,128)(2,1)}, f32[128,128]{1,0:T(8,128)}, f32[128,128]{1,0:T(8,128)}, f32[8,128]{1,0:T(8,128)}, f32[8,128]{1,0:T(8,128)}) custom-call(bf16[128,512]{1,0:T(8,128)(2,1)S(1)} %get-tuple-element.15.refs_0_, f32[128,128]{1,0:T(8,128)S(1)} %get-tuple-element.16.refs_1_, f32[128,128]{1,0:T(8,128)S(1)} %get-tuple-element.17.refs_2_, ...), custom_call_target="tpu_custom_call" | custom-call | tf_op jit(solution)/shard_map/pallas_call | solution.py:476

commit v3 on v2

--- a/solution.py
+++ b/solution.py
@@ -18,7 +18,7 @@
 STATE = 256
 CHUNK = 16
 CHUNKS = STATE // CHUNK
-NEAR_LAG = 1
+NEAR_LAG = 6
 
 
 def dot(a, b):
@@ -54,10 +54,10 @@
     igrad_ref, kgrad_ref, qgrad_ref, dgrad_ref, sgrad_ref,
     conv_ref, og_ref, k_ref, q_ref, ld_ref, ss_ref, skip_ref, cw_ref,
     pack, col_s, row_s, kp, qp, vhi, vlo, vals, dsilu, tsx, whi, wlo, shi, slo, within,
-    k_in, q_in, k_far, q_far, read_s, carried_s,
+    k_in, q_in, k_far, q_far, read_s, carried_s, out_acc, into_acc,
     lme, lsend, lother, tt, tlow, dme8, doth8, dchip8, dlow8, xin, xsend, xnear, xnsend, ebuf, epart,
-    ext, kpart, qpart, krecv, qrecv,
-    in_s, kq_ss, kq_rs, d_ss, d_rs, l_ss, l_rs, t_ss, t_rs, x_ss, x2_ss, x_rs, n_rs, e_ss, e_rs, f_ss, f_rs, c_ss, c_rs,
+    ext, kpart, qpart, krecv, qrecv, alpha, beta, alpha_r, beta_r, crow, k_top, kp_top,
+    in_s, kq_ss, kq_rs, d_ss, d_rs, l_ss, l_rs, t_ss, t_rs, x_ss, x2_ss, x_rs, n_rs, e_ss, e_rs, f_ss, f_rs, c_ss, c_rs, a_ss, a_rs,
 ):
     seq = lax.axis_index("seq")
     head = lax.axis_index("head")
@@ -69,8 +69,16 @@
     high = lax.rem(pos, 2) == 1
     low = lax.rem(pos, 2) == 0
     opens = group == 0
-    late = group >= chips // 4
-    sends_on = jnp.logical_and(high, group < chips // 2 - 1)
+    late = group >= 3 * chips // 8
+    middle = group >= chips // 4
+    last_group = chips // 2 - 1
+    closes = group == last_group
+    sends_on = jnp.logical_and(high, group < last_group)
+    sends_last = jnp.logical_and(high, group == last_group - 1)
+    sends_far = jnp.logical_and(high, group < last_group - 1)
+    inner = jnp.logical_not(opens)
+    takes32 = jnp.logical_and(inner, jnp.logical_and(high, jnp.logical_not(closes)))
+    takes16 = jnp.logical_and(inner, jnp.logical_or(low, closes))
     step1 = jnp.where(core == 0, 2, n_seq - 2)
     step2 = jnp.where(core == 0, 4, n_seq - 4)
 
@@ -80,13 +88,11 @@
     next1 = at(seq + step1)
     next2 = at(seq + step2)
     other_core = at(seq + 1 - 2 * core)
-    before = at(seq + n_seq - 1)
-    after_or_before = at(seq + jnp.where(core == 0, n_seq - 1, 1))
     partner = (seq, head + 1 - 2 * lax.rem(head, 2))
 
     barrier = pltpu.get_barrier_semaphore()
     greeted = (
-        at(seq + 2), at(seq + n_seq - 2), at(seq + 4), at(seq + n_seq - 4), other_core, after_or_before, partner,
+        at(seq + 2), at(seq + n_seq - 2), at(seq + 4), at(seq + n_seq - 4), other_core, partner,
     )
     for peer in greeted:
         pl.semaphore_signal(barrier, inc=1, device_id=peer, device_id_type=MESH)
@@ -105,6 +111,12 @@
         return pltpu.make_async_remote_copy(
             src_ref=src, dst_ref=dst, send_sem=ss, recv_sem=rs, device_id=peer, device_id_type=MESH
         )
+
+    pl.semaphore_wait(barrier, len(greeted))
+    k_copy = remote(k_hbm, kp, kq_ss.at[0], kq_rs.at[0], partner)
+    q_copy = remote(q_hbm, qp, kq_ss.at[1], kq_rs.at[1], partner)
+    k_copy.start()
+    q_copy.start()
 
     rows = iota((LEN, LEN), 0)
     cols = iota((LEN, LEN), 1)
@@ -138,11 +150,6 @@
     tsx[...] = dot(c_hi, ts_sel) + dot(c_lo, ts_sel)
     dme8[...] = jnp.broadcast_to(fsx[LEN - 1 : LEN, :], (8, WIDTH))
 
-    pl.semaphore_wait(barrier, len(greeted))
-    k_copy = remote(k_hbm, kp, kq_ss.at[0], kq_rs.at[0], partner)
-    q_copy = remote(q_hbm, qp, kq_ss.at[1], kq_rs.at[1], partner)
-    k_copy.start()
-    q_copy.start()
     d_copy = remote(dme8, doth8, d_ss.at[0], d_rs.at[0], other_core)
     d_copy.start()
 
@@ -177,21 +184,24 @@
 
     moves[4].wait()
     moves[5].wait()
-    local_half(0, k_ref[...], q_ref[...])
     k_copy.wait_recv()
     q_copy.wait_recv()
     local_half(1, kp[...], qp[...])
+    local_half(0, k_ref[...], q_ref[...])
     moves[6].wait()
     moves[7].wait()
 
     d_copy.wait_recv()
     dchip8[...] = dme8[...] * doth8[...]
 
+    def first_row(c):
+        return (c * CHUNK + HALF) % STATE
+
     def dt_copy():
         return remote(dchip8, dlow8, d_ss.at[1], d_rs.at[1], next1)
 
     def t_copy(c):
-        part = pl.ds(c * CHUNK, CHUNK)
+        part = pl.ds(first_row(c), CHUNK)
         return remote(tt.at[part], tlow.at[part], t_ss.at[c], t_rs.at[c], next1)
 
     @pl.when(low)
@@ -199,9 +209,9 @@
         dt_copy().start()
 
     for c in range(CHUNKS):
-        sl = slice(c * CHUNK, c * CHUNK + CHUNK)
+        sl = slice(first_row(c), first_row(c) + CHUNK)
         if c % (CHUNKS // 2) == 0:
-            l_copy(c // (CHUNKS // 2)).wait_recv()
+            l_copy(1 - c // (CHUNKS // 2)).wait_recv()
         tt[sl, :] = doth8[0:1, :] * lme[sl, :] + lother[sl, :]
 
         @pl.when(low)
@@ -217,61 +227,93 @@
     def _():
         xin[...] = jnp.zeros((STATE, WIDTH), F32)
 
-    def x_copy(c, far):
-        part = pl.ds(c * CHUNK, CHUNK)
-        if far:
-            return remote(xsend.at[part], xin.at[part], x2_ss.at[c], x_rs.at[c], next2)
+    def x_copy(c):
+        part = pl.ds(first_row(c), CHUNK)
+        return remote(xsend.at[part], xin.at[part], x2_ss.at[c], x_rs.at[c], next2)
+
+    def leaf_copy(c):
+        part = pl.ds(first_row(c), CHUNK)
         return remote(xnsend.at[part], xnear.at[part], x_ss.at[c], n_rs.at[c], next1)
 
+    def last_copy(c):
+        part = pl.ds(first_row(c), CHUNK)
+        return remote(xnsend.at[part], xnear.at[part], x2_ss.at[c], n_rs.at[c], next2)
+
     def e_copy(c):
-        part = pl.ds(c * CHUNK, CHUNK)
+        part = pl.ds(first_row(c), CHUNK)
         return remote(epart.at[part], ebuf.at[core, part], e_ss.at[c], e_rs.at[c], other_core)
 
-    def chain():
-        @pl.when(high)
-        def _():
-            dt_copy().wait_recv()
+    def chain(half):
+        if half == 0:
+
+            @pl.when(high)
+            def _():
+                dt_copy().wait_recv()
 
         a = dlow8[0:1, :]
         dchip = dchip8[0:1, :]
         dd = dchip * a
         dm = dme8[0:1, :]
+
         def forward_chunk(c):
-            sl = slice(c * CHUNK, c * CHUNK + CHUNK)
+            sl = slice(first_row(c), first_row(c) + CHUNK)
 
             @pl.when(high)
             def _():
                 t_copy(c).wait_recv()
 
-            @pl.when(jnp.logical_and(high, jnp.logical_not(opens)))
-            def _():
-                x_copy(c, True).wait_recv()
-
-            @pl.when(jnp.logical_and(low, jnp.logical_not(opens)))
-            def _():
-                x_copy(c, False).wait_recv()
+            @pl.when(takes32)
+            def _():
+                x_copy(c).wait_recv()
+
+            @pl.when(takes16)
+            def _():
+                leaf_copy(c).wait_recv()
                 xin[sl, :] = xnear[sl, :].astype(F32)
 
-            @pl.when(sends_on)
-            def _():
-                xsend[sl, :] = dd * xin[sl, :] + (dchip * tlow[sl, :] + tt[sl, :])
-                x_copy(c, True).start()
-                xnsend[sl, :] = xsend[sl, :].astype(BF16)
+            @pl.when(sends_far)
+            def _():
+                x = dd * xin[sl, :] + (dchip * tlow[sl, :] + tt[sl, :])
+                xsend[sl, :] = x
+                x_copy(c).start()
+                xnsend[sl, :] = x.astype(BF16)
+
+            @pl.when(sends_last)
+            def _():
+                x = dd * xin[sl, :] + (dchip * tlow[sl, :] + tt[sl, :])
+                xnsend[sl, :] = x.astype(BF16)
+                last_copy(c).start()
+                leaf_copy(c).start()
 
         def use_chunk(c):
-            sl = slice(c * CHUNK, c * CHUNK + CHUNK)
+            sl = slice(first_row(c), first_row(c) + CHUNK)
             em = a * xin[sl, :] + tlow[sl, :]
             ebuf[core, sl, :] = em
             epart[sl, :] = dm * em + lme[sl, :]
             e_copy(c).start()
 
-        for c in range(CHUNKS + NEAR_LAG):
-            if c < CHUNKS:
-                forward_chunk(c)
+        start, stop = (0, CHUNKS // 2) if half == 0 else (CHUNKS // 2, CHUNKS)
+        for c in range(start, stop):
+            forward_chunk(c)
             if c >= NEAR_LAG:
-                pl.when(sends_on)(x_copy(c - NEAR_LAG, False).start)
-            if 1 <= c <= CHUNKS:
+                pl.when(sends_far)(leaf_copy(c - NEAR_LAG).start)
+            if c > start:
                 use_chunk(c - 1)
+        if half == 1:
+
+            @pl.when(sends_far)
+            def _():
+                for c in range(CHUNKS - NEAR_LAG, CHUNKS):
+                    leaf_copy(c).start()
+
+        use_chunk(stop - 1)
+
+    ahead = [
+        remote(src, dst, a_ss.at[n], a_rs.at[n], other_core)
+        for n, (src, dst) in enumerate((
+            (alpha, alpha_r), (beta, beta_r), (k_ref.at[pl.ds(0, 16)], k_top), (kp.at[pl.ds(0, 16)], kp_top),
+        ))
+    ]
 
     def inside():
         scores = dot_t(k_ref[...], q_ref[...]) + dot_t(kp[...], qp[...])
@@ -309,60 +351,101 @@
         sk_hi, sk_lo = split2(skips)
         skip_row = (dot(sk_hi, heads_rows) + dot(sk_lo, heads_rows))[0:1, :]
         within[...] = within[...] + skip_row * og_ref[...].astype(F32)
+        alpha[...] = within[0:8, :] * dsilu[0:8, :]
+        beta[...] = tsx[0:8, :] * dsilu[0:8, :]
+
+        @pl.when(core == 0)
+        def _():
+            for move in ahead:
+                move.start()
 
     k_back = remote(kpart, krecv, f_ss.at[0], f_rs.at[0], partner)
     q_back = remote(qpart, qrecv, f_ss.at[1], f_rs.at[1], partner)
-    c_copy = remote(ext.at[pl.ds(0, 8)], ext.at[pl.ds(LEN, 8)], c_ss.at[0], c_rs.at[0], before)
+    c_far = remote(crow, ext.at[pl.ds(LEN, 8)], c_ss.at[0], c_rs.at[0], next1)
+    c_near = remote(ext.at[pl.ds(0, 8)], ext.at[pl.ds(LEN, 8)], c_ss.at[1], c_rs.at[1], other_core)
+    sends_rows = jnp.logical_and(core == 1, chip > 0)
+    takes_rows = jnp.logical_and(core == 1, chip < chips - 1)
 
     def both(a, b):
         return dot(a, b[0]) + dot(a, b[1])
 
-    def with_entering():
-        @pl.when(core == 1)
+    def their_chunks(of_core, half):
+        @pl.when(core == of_core)
         def _():
-            for c in range(CHUNKS):
+            for c in range(half * (CHUNKS // 2), (half + 1) * (CHUNKS // 2)):
                 e_copy(c).wait_recv()
 
+    def entering_far():
+        their_chunks(1, 0)
         far = split2(ebuf[0, HALF:, :])
         qpart[...] = (q_far[...] + dot_t(shi[...], far[0])).astype(BF16)
         q_back.start()
+        out_acc[...] = both(qp[...], far)
+
+    def entering_own():
+        their_chunks(1, 1)
         own = split2(ebuf[0, 0:HALF, :])
-        out_of = both(q_ref[...], own) + both(qp[...], far)
+        out_of = out_acc[...] + both(q_ref[...], own)
         read_s[...] = by_head(og_ref[...].astype(F32) * out_of)
         q_in[...] = q_in[...] + dot_t(shi[...], own[0])
 
-    def with_arriving():
-        @pl.when(core == 0)
-        def _():
-            for c in range(CHUNKS):
-                e_copy(c).wait_recv()
-
+    def arriving_far():
+        their_chunks(0, 0)
         far = split2(ebuf[1, HALF:, :])
         kpart[...] = (k_far[...] + dot_t(whi[...], far[0])).astype(BF16)
         k_back.start()
+        into_acc[...] = both(kp[...], far)
+
+    def arriving_own():
+        their_chunks(0, 1)
         own = split2(ebuf[1, 0:HALF, :])
-        into = both(k_ref[...], own) + both(kp[...], far)
+
+        @pl.when(core == 1)
+        def _():
+            for move in ahead:
+                move.wait_recv()
+            rows_of = both(k_top[...], split2(epart[0:HALF, :])) + both(kp_top[...], split2(epart[HALF:, :]))
+            crow[...] = alpha_r[...] + beta_r[...] * rows_of[0:8, :]
+            pl.when(sends_rows)(c_far.start)
+
+        into = into_acc[...] + both(k_ref[...], own)
         ext[0:LEN, :] = (within[...] + tsx[...] * into) * dsilu[...]
-
-        @pl.when(seq > 0)
-        def _():
-            c_copy.start()
-
+        pl.when(core == 1)(c_near.start)
         carried_s[...] = by_head(vals[...] * into)
         k_in[...] = k_in[...] + dot_t(whi[...], own[0])
 
-    mine = jnp.where(forward, 2, 3)
-    theirs = 5 - mine
+    parts = (
+        inside, functools.partial(chain, 0), functools.partial(chain, 1),
+        entering_far, entering_own, arriving_far, arriving_own,
+    )
+    mine = jnp.where(forward, 3, 5)
+    theirs = 8 - mine
 
     def turn(i, carry):
-        early = jnp.where(i < 2, jnp.where(jnp.logical_xor(i == 0, opens), 1, 0), jnp.where(i == 2, mine, theirs))
-        later = jnp.where(i == 0, 1, jnp.where(i == 1, theirs, jnp.where(i == 2, 0, mine)))
-        what = jnp.where(late, later, early)
-        for n, part in enumerate((chain, inside, with_entering, with_arriving)):
+        def pick(*order):
+            what = jnp.int32(0)
+            for n, part in enumerate(order):
+                what = jnp.where(i == n, part, what)
+            return what
+
+        what = jnp.where(
+            opens, pick(1, 2, 0, mine, mine + 1, theirs, theirs + 1),
+            jnp.where(
+                closes, pick(0, theirs, theirs + 1, 1, mine, 2, mine + 1),
+                jnp.where(
+                    late, pick(0, theirs, theirs + 1, 1, 2, mine, mine + 1),
+                    jnp.where(
+                        middle, pick(0, 1, 2, theirs, theirs + 1, mine, mine + 1),
+                        pick(0, 1, 2, mine, mine + 1, theirs, theirs + 1),
+                    ),
+                ),
+            ),
+        )
+        for n, part in enumerate(parts):
             pl.when(what == n)(part)
         return carry
 
-    lax.fori_loop(0, 4, turn, 0)
+    lax.fori_loop(0, len(parts), turn, 0)
 
     @pl.when(seq == n_seq - 1)
     def _():
@@ -380,19 +463,22 @@
     decay = dot(lh, since) + dot(ll, since) + dot(eh, strict) + dot(el, strict)
     dgrad_ref[...] = decay + jnp.exp(total) * cross
 
-    @pl.when(seq < n_seq - 1)
-    def _():
-        c_copy.wait_recv()
-
-    acc = cw_ref[3:4, :] * ext[0:LEN, :]
-    for tap in range(3):
-        acc = acc + cw_ref[tap : tap + 1, :] * ext[3 - tap : 3 - tap + LEN, :]
-    igrad_ref[...] = acc.astype(BF16)
+    def convolve(first, stop):
+        acc = cw_ref[3:4, :] * ext[first:stop, :]
+        for tap in range(3):
+            acc = acc + cw_ref[tap : tap + 1, :] * ext[first + 3 - tap : stop + 3 - tap, :]
+        igrad_ref[first:stop, :] = acc.astype(BF16)
+
+    convolve(0, LEN - 16)
 
     k_back.wait_recv()
     kgrad_ref[...] = k_in[...] + krecv[...].astype(F32)
     q_back.wait_recv()
     qgrad_ref[...] = q_in[...] + qrecv[...].astype(F32)
+
+    pl.when(core == 0)(c_near.wait_recv)
+    pl.when(takes_rows)(c_far.wait_recv)
+    convolve(LEN - 16, LEN)
 
     k_copy.wait_send()
     q_copy.wait_send()
@@ -409,17 +495,30 @@
     @pl.when(sends_on)
     def _():
         for c in range(CHUNKS):
-            x_copy(c, True).wait_send()
-            x_copy(c, False).wait_send()
+            leaf_copy(c).wait_send()
+
+    @pl.when(sends_far)
+    def _():
+        for c in range(CHUNKS):
+            x_copy(c).wait_send()
+
+    @pl.when(sends_last)
+    def _():
+        for c in range(CHUNKS):
+            last_copy(c).wait_send()
 
     for c in range(CHUNKS):
         e_copy(c).wait_send()
     k_back.wait_send()
     q_back.wait_send()
 
-    @pl.when(seq > 0)
-    def _():
-        c_copy.wait_send()
+    @pl.when(core == 0)
+    def _():
+        for move in ahead:
+            move.wait_send()
+
+    pl.when(core == 1)(c_near.wait_send)
+    pl.when(sends_rows)(c_far.wait_send)
 
 
 def store_kernel(*refs):
@@ -455,15 +554,18 @@
             vmem(tok, BF16), vmem(tok, BF16), vmem(tok, F32), vmem(tok, F32), vmem(tok, F32),
             vmem(tok, BF16), vmem(tok, BF16), vmem(tok, BF16), vmem(tok, BF16), vmem(tok, F32),
             vmem(sq, F32), vmem(sq, F32), vmem(sq, F32), vmem(sq, F32), vmem(small, F32), vmem(small, F32),
+            vmem(tok, F32), vmem(tok, F32),
             vmem(big, F32), vmem(big, F32), vmem(big, F32),
             vmem(big, F32), vmem(big, F32),
             vmem(row, F32), vmem(row, F32), vmem(row, F32), vmem(row, F32),
             vmem(big, F32), vmem(big, F32), vmem(big, BF16), vmem(big, BF16), vmem((2,) + big, F32), vmem(big, F32),
             vmem((LEN + 8, WIDTH), F32), vmem(sq, BF16), vmem(sq, BF16), vmem(sq, BF16), vmem(sq, BF16),
+            vmem(row, F32), vmem(row, F32), vmem(row, F32), vmem(row, F32), vmem(row, F32),
+            vmem((16, LEN), BF16), vmem((16, LEN), BF16),
             dma((8,)), dma((2,)), dma((2,)), dma((2,)), dma((2,)), dma((2,)), dma((2,)),
             dma((CHUNKS,)), dma((CHUNKS,)),
             dma((CHUNKS,)), dma((CHUNKS,)), dma((CHUNKS,)), dma((CHUNKS,)), dma((CHUNKS,)), dma((CHUNKS,)),
-            dma((2,)), dma((2,)), dma((1,)), dma((1,)),
+            dma((2,)), dma((2,)), dma((2,)), dma((2,)), dma((4,)), dma((4,)),
         ],
         compiler_params=pltpu.CompilerParams(
             collective_id=0, has_side_effects=True, vmem_limit_bytes=VMEM_BYTES

time: 62.3 us -> 54.3 us (0.87)
  Pallas kernels: 61.5 us -> 53.5 us
    pallas_call x1, Pallas kernels: 60.7 us -> 52.8 us  [body(): pl.pallas_call(functools.partial(kernel, n_seq), out_shape=tuple((vmem(o....]
where the time goes in v3:
time: 54.3 us; the launch traced here: 54.2 us
  Pallas kernels  53.5 us (99%)
  between operations  0.64 us (1%)
    pallas_call x1, Pallas kernels, body(): pl.pallas_call(functools.partial(kernel, n_seq), out_shape=tuple((vmem(o....  52.8 us

profile of v3, /device:TPU:1, one launch (start us, length us, event | category | flops | bytes accessed | tf_op | source)
XLA Modules:
  0.0 54.2 jit_solution(4091981389219164032)
XLA Ops:
  0.6 52.8 %shard_map.119 = (bf16[128,512]{1,0:T(8,128)(2,1)S(1)}, f32[128,128]{1,0:T(8,128)S(1)}, f32[128,128]{1,0:T(8,128)S(1)}, f32[8,128]{1,0:T(8,128)S(1)}, f32[8,128]{1,0:T(8,128)S(1)}) custom-call(bf16[128,512]{1,0:T(8,128)(2,1)} %conv_hbm.1, bf16[128,512]{1,0:T(8,128)(2,1)} %og_hbm.1, bf16[128,128]{1,0:T(8,128)(2,1)} %k_hbm.1, bf16[128,128]{1,0:T(8,128)(2,1)} %q_hbm.1, ...), custom_call_target="tpu_custom_call" | custom-call | flops 300000000 | bytes 1000000 | tf_op jit(solution)/shard_map/pallas_call | solution.py:545
  53.4 0.7 %shard_map.120 = (bf16[128,512]{1,0:T(8,128)(2,1)}, f32[128,128]{1,0:T(8,128)}, f32[128,128]{1,0:T(8,128)}, f32[8,128]{1,0:T(8,128)}, f32[8,128]{1,0:T(8,128)}) custom-call(bf16[128,512]{1,0:T(8,128)(2,1)S(1)} %get-tuple-element.15.refs_0_, f32[128,128]{1,0:T(8,128)S(1)} %get-tuple-element.16.refs_1_, f32[128,128]{1,0:T(8,128)S(1)} %get-tuple-element.17.refs_2_, ...), custom_call_target="tpu_custom_call" | custom-call | tf_op jit(solution)/shard_map/pallas_call | solution.py:578

commit v4 on v3

--- a/solution.py
+++ b/solution.py
@@ -19,6 +19,9 @@
 CHUNK = 16
 CHUNKS = STATE // CHUNK
 NEAR_LAG = 6
+PIECE = 4
+HEAD_CHUNKS = HALF // 2 // CHUNK
+FAR_DONE = CHUNKS - HEAD_CHUNKS
 
 
 def dot(a, b):
@@ -56,8 +59,9 @@
     pack, col_s, row_s, kp, qp, vhi, vlo, vals, dsilu, tsx, whi, wlo, shi, slo, within,
     k_in, q_in, k_far, q_far, read_s, carried_s, out_acc, into_acc,
     lme, lsend, lother, tt, tlow, dme8, doth8, dchip8, dlow8, xin, xsend, xnear, xnsend, ebuf, epart,
-    ext, kpart, qpart, krecv, qrecv, alpha, beta, alpha_r, beta_r, crow, k_top, kp_top,
+    ext, kpart, qpart, krecv, qrecv, alpha, beta, alpha_r, beta_r, crow, crow16, k_top, kp_top, us, ubuf, dgroup8, dbuf, weight,
     in_s, kq_ss, kq_rs, d_ss, d_rs, l_ss, l_rs, t_ss, t_rs, x_ss, x2_ss, x_rs, n_rs, e_ss, e_rs, f_ss, f_rs, c_ss, c_rs, a_ss, a_rs,
+    u_ss, u_rs, w_ss, w_rs,
 ):
     seq = lax.axis_index("seq")
     head = lax.axis_index("head")
@@ -71,13 +75,19 @@
     opens = group == 0
     late = group >= 3 * chips // 8
     middle = group >= chips // 4
-    last_group = chips // 2 - 1
+    groups = chips // 2
+    last_group = groups - 1 - core
     closes = group == last_group
+    at_end = group == groups - 1
+    backward = core == 1
+    gathers = jnp.logical_and(backward, jnp.logical_and(high, at_end))
+    gives = jnp.logical_and(backward, jnp.logical_and(high, group < groups - 1))
+    gives_first = jnp.logical_and(gives, group >= 2)
     sends_on = jnp.logical_and(high, group < last_group)
     sends_last = jnp.logical_and(high, group == last_group - 1)
     sends_far = jnp.logical_and(high, group < last_group - 1)
     inner = jnp.logical_not(opens)
-    takes32 = jnp.logical_and(inner, jnp.logical_and(high, jnp.logical_not(closes)))
+    takes32 = jnp.logical_and(inner, jnp.logical_and(high, jnp.logical_not(jnp.logical_or(closes, gathers))))
     takes16 = jnp.logical_and(inner, jnp.logical_or(low, closes))
     step1 = jnp.where(core == 0, 2, n_seq - 2)
     step2 = jnp.where(core == 0, 4, n_seq - 4)
@@ -112,7 +122,14 @@
             src_ref=src, dst_ref=dst, send_sem=ss, recv_sem=rs, device_id=peer, device_id_type=MESH
         )
 
-    pl.semaphore_wait(barrier, len(greeted))
+    @pl.when(gathers)
+    def _():
+        for z in range(4, chips - 2, 2):
+            pl.semaphore_signal(barrier, inc=1, device_id=(2 * z + 1, head), device_id_type=MESH)
+
+    far_giver = jnp.logical_and(gives, jnp.logical_and(chip >= 4, chip < chips - 2))
+    pl.semaphore_wait(barrier, len(greeted) + jnp.where(far_giver, 1, 0))
+
     k_copy = remote(k_hbm, kp, kq_ss.at[0], kq_rs.at[0], partner)
     q_copy = remote(q_hbm, qp, kq_ss.at[1], kq_rs.at[1], partner)
     k_copy.start()
@@ -184,10 +201,10 @@
 
     moves[4].wait()
     moves[5].wait()
+    local_half(0, k_ref[...], q_ref[...])
     k_copy.wait_recv()
     q_copy.wait_recv()
     local_half(1, kp[...], qp[...])
-    local_half(0, k_ref[...], q_ref[...])
     moves[6].wait()
     moves[7].wait()
 
@@ -195,7 +212,11 @@
     dchip8[...] = dme8[...] * doth8[...]
 
     def first_row(c):
-        return (c * CHUNK + HALF) % STATE
+        if c < HEAD_CHUNKS:
+            return c * CHUNK
+        if c < FAR_DONE:
+            return HALF + (c - HEAD_CHUNKS) * CHUNK
+        return (c - HALF // CHUNK) * CHUNK
 
     def dt_copy():
         return remote(dchip8, dlow8, d_ss.at[1], d_rs.at[1], next1)
@@ -210,8 +231,10 @@
 
     for c in range(CHUNKS):
         sl = slice(first_row(c), first_row(c) + CHUNK)
-        if c % (CHUNKS // 2) == 0:
-            l_copy(1 - c // (CHUNKS // 2)).wait_recv()
+        if c == 0:
+            l_copy(0).wait_recv()
+        if c == HEAD_CHUNKS:
+            l_copy(1).wait_recv()
         tt[sl, :] = doth8[0:1, :] * lme[sl, :] + lother[sl, :]
 
         @pl.when(low)
@@ -235,6 +258,37 @@
         part = pl.ds(first_row(c), CHUNK)
         return remote(xnsend.at[part], xnear.at[part], x_ss.at[c], n_rs.at[c], next1)
 
+    def u_copy(g, p):
+        part = pl.ds(first_row(p * PIECE), PIECE * CHUNK)
+        return remote(us.at[part], ubuf.at[g, part], u_ss.at[p], u_rs.at[g, p], (1, head))
+
+    def w_copy(g):
+        return remote(dgroup8, dbuf.at[g], w_ss.at[0], w_rs.at[g], (1, head))
+
+    def back_copy(c):
+        part = pl.ds(first_row(c), CHUNK)
+        return remote(xnsend.at[part], xnear.at[part], x_ss.at[c], n_rs.at[c], at(seq + 2))
+
+    def give():
+        @pl.when(gives)
+        def _():
+            @pl.when(gives_first)
+            def _():
+                dt_copy().wait_recv()
+
+            dchip = dchip8[0:1, :]
+            dgroup8[...] = dchip8[...] * dlow8[...]
+            w_copy(group).start()
+            for p in range(CHUNKS // PIECE):
+                @pl.when(gives_first)
+                def _():
+                    for c in range(p * PIECE, p * PIECE + PIECE):
+                        t_copy(c).wait_recv()
+
+                sl = slice(first_row(p * PIECE), first_row(p * PIECE) + PIECE * CHUNK)
+                us[sl, :] = (dchip * tlow[sl, :] + tt[sl, :]).astype(BF16)
+                u_copy(group, p).start()
+
     def last_copy(c):
         part = pl.ds(first_row(c), CHUNK)
         return remote(xnsend.at[part], xnear.at[part], x2_ss.at[c], n_rs.at[c], next2)
@@ -246,9 +300,18 @@
     def chain(half):
         if half == 0:
 
-            @pl.when(high)
+            @pl.when(jnp.logical_and(high, jnp.logical_not(gives_first)))
             def _():
                 dt_copy().wait_recv()
+
+            @pl.when(gathers)
+            def _():
+                for g in range(groups - 1):
+                    w_copy(g).wait_recv()
+                share = jnp.ones((1, WIDTH), F32)
+                for g in range(groups - 2, -1, -1):
+                    weight[g : g + 1, :] = share
+                    share = share * dbuf[g, 0:1, :]
 
         a = dlow8[0:1, :]
         dchip = dchip8[0:1, :]
@@ -258,9 +321,21 @@
         def forward_chunk(c):
             sl = slice(first_row(c), first_row(c) + CHUNK)
 
-            @pl.when(high)
+            @pl.when(jnp.logical_and(high, jnp.logical_not(gives_first)))
             def _():
                 t_copy(c).wait_recv()
+
+            @pl.when(gathers)
+            def _():
+                if c % PIECE == 0:
+                    for g in range(groups - 1):
+                        u_copy(g, c // PIECE).wait_recv()
+                x = weight[0:1, :] * ubuf[0, sl, :].astype(F32)
+                for g in range(1, groups - 1):
+                    x = x + weight[g : g + 1, :] * ubuf[g, sl, :].astype(F32)
+                xin[sl, :] = x
+                xnsend[sl, :] = x.astype(BF16)
+                back_copy(c).start()
 
             @pl.when(takes32)
             def _():
@@ -292,7 +367,7 @@
             epart[sl, :] = dm * em + lme[sl, :]
             e_copy(c).start()
 
-        start, stop = (0, CHUNKS // 2) if half == 0 else (CHUNKS // 2, CHUNKS)
+        start, stop = (0, FAR_DONE) if half == 0 else (FAR_DONE, CHUNKS)
         for c in range(start, stop):
             forward_chunk(c)
             if c >= NEAR_LAG:
@@ -372,7 +447,7 @@
     def their_chunks(of_core, half):
         @pl.when(core == of_core)
         def _():
-            for c in range(half * (CHUNKS // 2), (half + 1) * (CHUNKS // 2)):
+            for c in range(0, FAR_DONE) if half == 0 else range(FAR_DONE, CHUNKS):
                 e_copy(c).wait_recv()
 
     def entering_far():
@@ -396,15 +471,19 @@
         k_back.start()
         into_acc[...] = both(kp[...], far)
 
-    def arriving_own():
-        their_chunks(0, 1)
-        own = split2(ebuf[1, 0:HALF, :])
-
         @pl.when(core == 1)
         def _():
             for move in ahead:
                 move.wait_recv()
-            rows_of = both(k_top[...], split2(epart[0:HALF, :])) + both(kp_top[...], split2(epart[HALF:, :]))
+            crow16[...] = both(kp_top[...], split2(epart[HALF:, :]))
+
+    def arriving_own():
+        their_chunks(0, 1)
+        own = split2(ebuf[1, 0:HALF, :])
+
+        @pl.when(core == 1)
+        def _():
+            rows_of = both(k_top[...], split2(epart[0:HALF, :])) + crow16[...]
             crow[...] = alpha_r[...] + beta_r[...] * rows_of[0:8, :]
             pl.when(sends_rows)(c_far.start)
 
@@ -416,7 +495,7 @@
 
     parts = (
         inside, functools.partial(chain, 0), functools.partial(chain, 1),
-        entering_far, entering_own, arriving_far, arriving_own,
+        entering_far, entering_own, arriving_far, arriving_own, give,
     )
     mine = jnp.where(forward, 3, 5)
     theirs = 8 - mine
@@ -429,14 +508,17 @@
             return what
 
         what = jnp.where(
-            opens, pick(1, 2, 0, mine, mine + 1, theirs, theirs + 1),
+            opens, pick(1, 2, 7, 0, mine, mine + 1, theirs, theirs + 1),
             jnp.where(
-                closes, pick(0, theirs, theirs + 1, 1, mine, 2, mine + 1),
+                jnp.logical_or(closes, at_end), pick(0, 7, theirs, theirs + 1, 1, mine, 2, mine + 1),
                 jnp.where(
-                    late, pick(0, theirs, theirs + 1, 1, 2, mine, mine + 1),
+                    late, pick(0, 7, theirs, theirs + 1, 1, 2, mine, mine + 1),
                     jnp.where(
-                        middle, pick(0, 1, 2, theirs, theirs + 1, mine, mine + 1),
-                        pick(0, 1, 2, mine, mine + 1, theirs, theirs + 1),
+                        middle, pick(0, 7, 1, 2, theirs, theirs + 1, mine, mine + 1),
+                        jnp.where(
+                            group == 1, pick(0, 1, 2, 7, mine, mine + 1, theirs, theirs + 1),
+                            pick(0, 7, 1, 2, mine, mine + 1, theirs, theirs + 1),
+                        ),
                     ),
                 ),
             ),
@@ -471,15 +553,6 @@
 
     convolve(0, LEN - 16)
 
-    k_back.wait_recv()
-    kgrad_ref[...] = k_in[...] + krecv[...].astype(F32)
-    q_back.wait_recv()
-    qgrad_ref[...] = q_in[...] + qrecv[...].astype(F32)
-
-    pl.when(core == 0)(c_near.wait_recv)
-    pl.when(takes_rows)(c_far.wait_recv)
-    convolve(LEN - 16, LEN)
-
     k_copy.wait_send()
     q_copy.wait_send()
     d_copy.wait_send()
@@ -509,6 +582,26 @@
 
     for c in range(CHUNKS):
         e_copy(c).wait_send()
+    @pl.when(gives)
+    def _():
+        w_copy(group).wait_send()
+        for p in range(CHUNKS // PIECE):
+            u_copy(group, p).wait_send()
+
+    @pl.when(gathers)
+    def _():
+        for c in range(CHUNKS):
+            back_copy(c).wait_send()
+
+    k_back.wait_recv()
+    kgrad_ref[...] = k_in[...] + krecv[...].astype(F32)
+    q_back.wait_recv()
+    qgrad_ref[...] = q_in[...] + qrecv[...].astype(F32)
+
+    pl.when(core == 0)(c_near.wait_recv)
+    pl.when(takes_rows)(c_far.wait_recv)
+    convolve(LEN - 16, LEN)
+
     k_back.wait_send()
     q_back.wait_send()
 
@@ -539,6 +632,7 @@
     sq = (LEN, LEN)
     small = (HEADS, LEN)
     row = (8, WIDTH)
+    gmax = n_seq // 4 - 1
     in_vmem = pl.BlockSpec(memory_space=vmem)
     hbm = pl.BlockSpec(memory_space=pltpu.HBM)
     outs = (shape(tok, BF16), shape(sq, F32), shape(sq, F32), shape(small, F32), shape(small, F32))
@@ -561,11 +655,13 @@
             vmem(big, F32), vmem(big, F32), vmem(big, BF16), vmem(big, BF16), vmem((2,) + big, F32), vmem(big, F32),
             vmem((LEN + 8, WIDTH), F32), vmem(sq, BF16), vmem(sq, BF16), vmem(sq, BF16), vmem(sq, BF16),
             vmem(row, F32), vmem(row, F32), vmem(row, F32), vmem(row, F32), vmem(row, F32),
-            vmem((16, LEN), BF16), vmem((16, LEN), BF16),
+            vmem((16, WIDTH), F32), vmem((16, LEN), BF16), vmem((16, LEN), BF16),
+            vmem(big, BF16), vmem((gmax,) + big, BF16), vmem(row, F32), vmem((gmax,) + row, F32), vmem((8, WIDTH), F32),
             dma((8,)), dma((2,)), dma((2,)), dma((2,)), dma((2,)), dma((2,)), dma((2,)),
             dma((CHUNKS,)), dma((CHUNKS,)),
             dma((CHUNKS,)), dma((CHUNKS,)), dma((CHUNKS,)), dma((CHUNKS,)), dma((CHUNKS,)), dma((CHUNKS,)),
             dma((2,)), dma((2,)), dma((2,)), dma((2,)), dma((4,)), dma((4,)),
+            dma((CHUNKS // PIECE,)), dma((gmax, CHUNKS // PIECE)), dma((1,)), dma((gmax,)),
         ],
         compiler_params=pltpu.CompilerParams(
             collective_id=0, has_side_effects=True, vmem_limit_bytes=VMEM_BYTES

time: 54.3 us -> 48.1 us (0.89)
  the two profiles are of different devices: /device:TPU:1 before, /device:TPU:35 now
where the time goes in v4:
time: 48.1 us; the launch traced here: 48 us
  Pallas kernels  47.4 us (99%)
  between operations  0.64 us (1%)
    pallas_call x1, Pallas kernels, body(): pl.pallas_call(functools.partial(kernel, n_seq), out_shape=tuple((vmem(o....  46.6 us

profile of v4, /device:TPU:35, one launch (start us, length us, event | category | flops | bytes accessed | tf_op | source)
XLA Modules:
  0.0 48.0 jit_solution(13106005469411813044)
XLA Ops:
  0.6 46.6 %shard_map.119 = (bf16[128,512]{1,0:T(8,128)(2,1)S(1)}, f32[128,128]{1,0:T(8,128)S(1)}, f32[128,128]{1,0:T(8,128)S(1)}, f32[8,128]{1,0:T(8,128)S(1)}, f32[8,128]{1,0:T(8,128)S(1)}) custom-call(bf16[128,512]{1,0:T(8,128)(2,1)} %conv_hbm.1, bf16[128,512]{1,0:T(8,128)(2,1)} %og_hbm.1, bf16[128,128]{1,0:T(8,128)(2,1)} %k_hbm.1, bf16[128,128]{1,0:T(8,128)(2,1)} %q_hbm.1, ...), custom_call_target="tpu_custom_call" | custom-call | flops 300000000 | bytes 1000000 | tf_op jit(solution)/shard_map/pallas_call | solution.py:639
  47.3 0.7 %shard_map.120 = (bf16[128,512]{1,0:T(8,128)(2,1)}, f32[128,128]{1,0:T(8,128)}, f32[128,128]{1,0:T(8,128)}, f32[8,128]{1,0:T(8,128)}, f32[8,128]{1,0:T(8,128)}) custom-call(bf16[128,512]{1,0:T(8,128)(2,1)S(1)} %get-tuple-element.15.refs_0_, f32[128,128]{1,0:T(8,128)S(1)} %get-tuple-element.16.refs_1_, f32[128,128]{1,0:T(8,128)S(1)} %get-tuple-element.17.refs_2_, ...), custom_call_target="tpu_custom_call" | custom-call | tf_op jit(solution)/shard_map/pallas_call | solution.py:674

commit v5 on v4

--- a/solution.py
+++ b/solution.py
@@ -101,10 +101,18 @@
     partner = (seq, head + 1 - 2 * lax.rem(head, 2))
 
     barrier = pltpu.get_barrier_semaphore()
-    greeted = (
-        at(seq + 2), at(seq + n_seq - 2), at(seq + 4), at(seq + n_seq - 4), other_core, partner,
+    near = (
+        (seq + 2, chip < chips - 1), (seq + n_seq - 2, chip > 0), (seq + 4, chip < chips - 2), (seq + n_seq - 4, chip > 1),
     )
-    for peer in greeted:
+    greetings = jnp.int32(2)
+    for peer, there in near:
+        greetings = greetings + jnp.where(there, 1, 0)
+
+        @pl.when(there)
+        def _():
+            pl.semaphore_signal(barrier, inc=1, device_id=at(peer), device_id_type=MESH)
+
+    for peer in (other_core, partner):
         pl.semaphore_signal(barrier, inc=1, device_id=peer, device_id_type=MESH)
 
     moves = [
@@ -124,11 +132,11 @@
 
     @pl.when(gathers)
     def _():
-        for z in range(4, chips - 2, 2):
+        for z in range(4, chips, 2):
             pl.semaphore_signal(barrier, inc=1, device_id=(2 * z + 1, head), device_id_type=MESH)
 
-    far_giver = jnp.logical_and(gives, jnp.logical_and(chip >= 4, chip < chips - 2))
-    pl.semaphore_wait(barrier, len(greeted) + jnp.where(far_giver, 1, 0))
+    far_giver = jnp.logical_and(gives, chip >= 4)
+    pl.semaphore_wait(barrier, greetings + jnp.where(far_giver, 1, 0))
 
     k_copy = remote(k_hbm, kp, kq_ss.at[0], kq_rs.at[0], partner)
     q_copy = remote(q_hbm, qp, kq_ss.at[1], kq_rs.at[1], partner)
@@ -477,6 +485,12 @@
                 move.wait_recv()
             crow16[...] = both(kp_top[...], split2(epart[HALF:, :]))
 
+    def convolve(first, stop):
+        acc = cw_ref[3:4, :] * ext[first:stop, :]
+        for tap in range(3):
+            acc = acc + cw_ref[tap : tap + 1, :] * ext[first + 3 - tap : stop + 3 - tap, :]
+        igrad_ref[first:stop, :] = acc.astype(BF16)
+
     def arriving_own():
         their_chunks(0, 1)
         own = split2(ebuf[1, 0:HALF, :])
@@ -492,6 +506,7 @@
         pl.when(core == 1)(c_near.start)
         carried_s[...] = by_head(vals[...] * into)
         k_in[...] = k_in[...] + dot_t(whi[...], own[0])
+        convolve(0, LEN - 16)
 
     parts = (
         inside, functools.partial(chain, 0), functools.partial(chain, 1),
@@ -510,7 +525,7 @@
         what = jnp.where(
             opens, pick(1, 2, 7, 0, mine, mine + 1, theirs, theirs + 1),
             jnp.where(
-                jnp.logical_or(closes, at_end), pick(0, 7, theirs, theirs + 1, 1, mine, 2, mine + 1),
+                jnp.logical_or(closes, jnp.logical_and(at_end, jnp.logical_not(gathers))), pick(0, 7, theirs, theirs + 1, 1, mine, 2, mine + 1),
                 jnp.where(
                     late, pick(0, 7, theirs, theirs + 1, 1, 2, mine, mine + 1),
                     jnp.where(
@@ -544,14 +559,6 @@
     strict = flag(rows < cols)
     decay = dot(lh, since) + dot(ll, since) + dot(eh, strict) + dot(el, strict)
     dgrad_ref[...] = decay + jnp.exp(total) * cross
-
-    def convolve(first, stop):
-        acc = cw_ref[3:4, :] * ext[first:stop, :]
-        for tap in range(3):
-            acc = acc + cw_ref[tap : tap + 1, :] * ext[first + 3 - tap : stop + 3 - tap, :]
-        igrad_ref[first:stop, :] = acc.astype(BF16)
-
-    convolve(0, LEN - 16)
 
     k_copy.wait_send()
     q_copy.wait_send()

time: 48.1 us -> 48.4 us (level)
  the two profiles are of different devices: /device:TPU:35 before, /device:TPU:33 now
where the time goes in v5:
time: 48.4 us; the launch traced here: 48.2 us
  Pallas kernels  47.6 us (98%)
  between operations  0.64 us (1%)
    pallas_call x1, Pallas kernels, body(): pl.pallas_call(functools.partial(kernel, n_seq), out_shape=tuple((vmem(o....  46.8 us

profile of v5, /device:TPU:33, one launch (start us, length us, event | category | flops | bytes accessed | tf_op | source)
XLA Modules:
  0.0 48.2 jit_solution(16786469926522785011)
XLA Ops:
  0.6 46.8 %shard_map.119 = (bf16[128,512]{1,0:T(8,128)(2,1)S(1)}, f32[128,128]{1,0:T(8,128)S(1)}, f32[128,128]{1,0:T(8,128)S(1)}, f32[8,128]{1,0:T(8,128)S(1)}, f32[8,128]{1,0:T(8,128)S(1)}) custom-call(bf16[128,512]{1,0:T(8,128)(2,1)} %conv_hbm.1, bf16[128,512]{1,0:T(8,128)(2,1)} %og_hbm.1, bf16[128,128]{1,0:T(8,128)(2,1)} %k_hbm.1, bf16[128,128]{1,0:T(8,128)(2,1)} %q_hbm.1, ...), custom_call_target="tpu_custom_call" | custom-call | flops 300000000 | bytes 1000000 | tf_op jit(solution)/shard_map/pallas_call | solution.py:646
  47.5 0.7 %shard_map.120 = (bf16[128,512]{1,0:T(8,128)(2,1)}, f32[128,128]{1,0:T(8,128)}, f32[128,128]{1,0:T(8,128)}, f32[8,128]{1,0:T(8,128)}, f32[8,128]{1,0:T(8,128)}) custom-call(bf16[128,512]{1,0:T(8,128)(2,1)S(1)} %get-tuple-element.15.refs_0_, f32[128,128]{1,0:T(8,128)S(1)} %get-tuple-element.16.refs_1_, f32[128,128]{1,0:T(8,128)S(1)} %get-tuple-element.17.refs_2_, ...), custom_call_target="tpu_custom_call" | custom-call | tf_op jit(solution)/shard_map/pallas_call | solution.py:681
